TPU v7x, 256 devices: a whole 4x4x8 slice. The times are simulated.
256 devices in a mesh: group: 4 (over z_hi, core), fsdp: 64 (over y, z_lo, x).
Axes of the slice: x: 4, y: 4, z: 8 (z_hi: 2, z_lo: 4; z = z_hi * 4 + z_lo), core: 2. Of those that a mesh axis runs over, the one named last changes fastest.
Arguments:
- tokens: bfloat16 [768, 8192], P(('group', 'fsdp')), may hold values from -6 to 6
- gate_master: bfloat16 [8192, 26624], P('group', 'fsdp'), may hold values from -0.4087961 to 0.4087961
- up_master: bfloat16 [8192, 26624], P('group', 'fsdp'), may hold values from -0.4087961 to 0.4087961
- hidden_cotangent: bfloat16 [768, 26624], P('group', 'fsdp'), may hold values from -1.75 to 1.75
Outputs:
- hidden: bfloat16 [768, 26624], P('group', 'fsdp')
- token_grad: bfloat16 [768, 8192], P(('group', 'fsdp'))
- gate_grad: bfloat16 [8192, 26624], P('group', 'fsdp')
- up_grad: bfloat16 [8192, 26624], P('group', 'fsdp')
All inputs are finite; a program needn't handle non-finite values.
Results may differ from a plain program's by a relative error of at most 0.012.
Values may be sent and summed in bfloat16 or wider, within the bound.
A program may use at most 128 MiB of HBM per device.

v0:
```python
import jax
import jax.numpy as jnp
from jax import lax
from jax.sharding import PartitionSpec as P

QMAX = 60.0
EPS = 1e-06


def quantize(master, amax):
    factor = QMAX / (amax + EPS)
    scaled = master.astype(jnp.float32) * factor
    return jnp.floor(scaled + 0.5).astype(jnp.bfloat16)


def on_device(tokens, gate_master, up_master, hidden_cotangent):
    gate_amax, up_amax = lax.pmax(
        (
            jnp.max(jnp.abs(gate_master)).astype(jnp.float32),
            jnp.max(jnp.abs(up_master)).astype(jnp.float32),
        ),
        ("group", "fsdp"),
    )
    gate_quant, up_quant = (
        lax.all_gather(quantize(gate_master, gate_amax), "group", axis=0, tiled=True),
        lax.all_gather(quantize(up_master, up_amax), "group", axis=0, tiled=True),
    )
    gate_scale = (gate_amax + EPS) / QMAX
    up_scale = (up_amax + EPS) / QMAX
    grouped = lax.all_gather(tokens, "fsdp", axis=0, tiled=True)
    gate = jnp.dot(grouped, gate_quant, preferred_element_type=jnp.float32) * gate_scale
    up = jnp.dot(grouped, up_quant, preferred_element_type=jnp.float32) * up_scale
    sig = jax.nn.sigmoid(gate)
    silu = gate * sig
    hidden = (silu * up).astype(jnp.bfloat16)
    cotangent = hidden_cotangent.astype(jnp.float32)
    gate_act = (cotangent * up * sig * (1.0 + gate * (1.0 - sig))).astype(jnp.bfloat16)
    up_act = (cotangent * silu).astype(jnp.bfloat16)
    contract_last = (((1,), (1,)), ((), ()))
    term = (
        lax.dot_general(gate_act, gate_quant, contract_last, preferred_element_type=jnp.float32)
        * gate_scale
    )
    token_grad = lax.psum_scatter(
        term
        + lax.dot_general(up_act, up_quant, contract_last, preferred_element_type=jnp.float32)
        * up_scale,
        "fsdp",
        scatter_dimension=0,
        tiled=True,
    )
    both_acts = jnp.concatenate([gate_act, up_act], axis=1)
    summed = lax.psum_scatter(
        lax.dot_general(
            grouped, both_acts, (((0,), (0,)), ((), ())), preferred_element_type=jnp.float32
        ).astype(jnp.bfloat16),
        "group",
        scatter_dimension=0,
        tiled=True,
    ).astype(jnp.float32)
    split_at = gate_master.shape[1]
    return (
        hidden,
        token_grad.astype(jnp.bfloat16),
        summed[:, :split_at].astype(jnp.bfloat16),
        summed[:, split_at:].astype(jnp.bfloat16),
    )


def solution(mesh):
    placed = (
        P(("group", "fsdp"), None),
        P("group", "fsdp"),
        P("group", "fsdp"),
        P("group", "fsdp"),
    )
    return jax.shard_map(
        on_device,
        mesh=mesh,
        in_specs=placed,
        out_specs=(
            P("group", "fsdp"),
            P(("group", "fsdp"), None),
            P("group", "fsdp"),
            P("group", "fsdp"),
        ),
        check_vma=False,
    )
```

profile of v0, /device:TPU:0, one launch (start us, length us, event | category | flops | bytes accessed | tf_op | source)
XLA Modules:
  0.0 1092.8 jit_solution(4618680197450321585)
XLA Ops:
  7.2 0.0 all-gather.9.cloned.1.call-start
  7.2 0.7 all-gather.9.cloned.1.call-update
  7.9 0.0 all-gather.5.cloned.1.call-start
  8.0 3.2 abs_reduce_fusion
  11.2 80.7 %all-reduce.1 = (f32[]{:T(128)}, f32[]{:T(128)}) all-reduce(bf16[]{:T(256)} %get-tuple-element.11, bf16[]{:T(256)} %get-tuple-element.12), channel_id=1, replica_groups=mesh['group'=4,'fsdp'=64] {'group','fsdp'}, use_global_device_ids=true, to_apply=%region_3.0 | all-reduce | flops 2 | bytes 12 | tf_op jit(solution)/shard_map/pmax | solution.py:17
  92.5 1.7 floor_convert_fusion.1
  94.2 0.0 all-gather.5.cloned.1.call-update
  94.3 0.0 all-gather.7.cloned.1.call-start
  95.0 1.7 floor_convert_fusion
  96.7 0.2 reduce-scatter.2.cloned.1.call-start
  97.0 267.5 %all-gather.9.cloned.1.call-done = bf16[64,3,8192]{2,1,0:T(4,128)(2,1)} async-done(((bf16[1,3,8192]{2,1,0:T(4,128)(2,1)}), bf16[64,3,8192]{2,1,0:T(4,128)(2,1)}) %all-gather.9.cloned.1.call-update) | async-done | bytes 3145744 | tf_op jit(solution)/shard_map/all_gather | solution.py:30
  364.5 6.0 reshape.9
  370.5 90.4 %all-gather.5.cloned.1.call-done = bf16[8192,416]{0,1:T(8,128)(2,1)} async-done(((bf16[2048,416]{0,1:T(8,128)(2,1)}), bf16[8192,416]{0,1:T(8,128)(2,1)}) %all-gather.5.cloned.1.call-update) | async-done | bytes 6815760 | tf_op jit(solution)/shard_map/all_gather | solution.py:25
  460.9 5.9 fusion.3
  466.8 88.5 %all-gather.7.cloned.1.call-done = bf16[8192,416]{0,1:T(8,128)(2,1)} async-done(((bf16[2048,416]{0,1:T(8,128)(2,1)}), bf16[8192,416]{0,1:T(8,128)(2,1)}) %all-gather.7.cloned.1.call-update) | async-done | bytes 6815760 | tf_op jit(solution)/shard_map/all_gather | solution.py:26
  555.3 6.1 fusion.6
  561.4 7.3 fusion
  568.7 0.6 copy-done.2
  569.3 0.6 dynamic-slice
  570.5 4.9 convolution_multiply_fusion
  575.5 5.8 fusion.1
  581.3 500.1 %all-reduce.3 = bf16[192,8192]{1,0:T(8,128)(2,1)S(1)} all-reduce(f32[192,8192]{1,0:T(8,128)} %fusion.1), channel_id=2, replica_groups=mesh['group'=4,'fsdp'=64] {'fsdp'}, use_global_device_ids=true, to_apply=%region_4.0.clone | all-reduce | flops 1572864 | bytes 9437184
  1081.4 0.7 dynamic-slice_convert_fusion
  1082.1 4.2 fusion.13
  (13 shorter events, 0.1 us)
Async XLA Ops:
  7.2 85.4 %copy-start = (bf16[2048,416]{0,1:T(8,128)(2,1)S(1)}, bf16[2048,416]{0,1:T(8,128)(2,1)}, u32[]{:S(2)}) copy-start(bf16[2048,416]{0,1:T(8,128)(2,1)} %param.5) | copy-start | bytes 5111812
  7.2 357.4 %all-gather.9.cloned.1.call-start = ((), (), s32[]{:S(2)}) async-start(), calls=%async_computation.4 | async-start | bytes 4259840 | tf_op jit(solution)/shard_map/all_gather | solution.py:30
  7.9 453.0 %all-gather.5.cloned.1.call-start = ((), (), s32[]{:S(2)}) async-start(), calls=%async_computation.1 | async-start | bytes 8519680 | tf_op jit(solution)/shard_map/all_gather | solution.py:25
  11.2 83.8 %copy-start.1 = (bf16[2048,416]{0,1:T(8,128)(2,1)S(1)}, bf16[2048,416]{0,1:T(8,128)(2,1)}, u32[]{:S(2)}) copy-start(bf16[2048,416]{0,1:T(8,128)(2,1)} %param.6) | copy-start | bytes 5111812
  94.3 461.0 %all-gather.7.cloned.1.call-start = ((), (), s32[]{:S(2)}) async-start(), calls=%async_computation.2 | async-start | bytes 8519680 | tf_op jit(solution)/shard_map/all_gather | solution.py:26
  96.7 985.3 %reduce-scatter.2.cloned.1.call-start = ((), (), s32[]{:S(2)}) async-start(), calls=%async_computation.3 | async-start | bytes 17039360 | tf_op jit(solution)/shard_map/reduce_scatter | solution.py:53
  568.6 0.7 copy-start.2
  568.6 6.8 slice-start
  570.5 4.9 slice-start.1
Sparse Core Ops, SparseCore 0:
  9.8 354.6 all-gather.8
  366.9 93.9 all-gather.4
  463.3 91.9 all-gather.6
  568.8 225.1 reduce-scatter.1
where the time goes:
time: 1090 us
  blocking collectives  581 us (53%)
  waiting for transfers between devices  447 us (41%)
  matrix products  29.9 us (3%)
  between operations  15.9 us (1%)
  local copies, waits for them, and re-layouts  12.1 us (1%)
    unnamed x1, blocking collectives  500 us
    all_gather x1, waiting for transfers between devices, on_device(): grouped = lax.all_gather(tokens, 'fsdp', axis=0, tiled=True)  268 us
    all_gather x1, waiting for transfers between devices, on_device(): lax.all_gather(quantize(gate_master, gate_amax), 'group', axis=0, tiled=T...  90.4 us
    all_gather x1, waiting for transfers between devices, on_device(): lax.all_gather(quantize(up_master, up_amax), 'group', axis=0, tiled=True)  88.5 us
    pmax x1, blocking collectives, on_device(): lax.pmax((jnp.max(jnp.abs(gate_master)).astype(jnp.float32), jnp.max(jnp....  80.7 us
  transfers between devices with their start and end apart: 4, of which 3 were waited for; matrix products, arithmetic and copies ran while one was open for 3% of the time, Pallas kernels for 0%

commit v1 on v0

v1 whole, which is shorter than its diff:
```python
import functools

import jax
import jax.numpy as jnp
from jax import lax
from jax.experimental import pallas as pl
from jax.experimental.pallas import tpu as pltpu
from jax.sharding import PartitionSpec as P

QMAX = 60.0
EPS = 1e-06
MESH = pl.DeviceIdType.MESH
F32 = jnp.float32
BF16 = jnp.bfloat16

DQ = 2048
FW = 416
FA = 384
FT = FW - FA
FP = 896
ORDER = (1, 3, 2)


def position():
    g = lax.axis_index("group")
    f = lax.axis_index("fsdp")
    return lax.div(g, 2), lax.rem(g, 2), lax.div(f, 16), lax.rem(lax.div(f, 4), 4), lax.rem(f, 4)


def place(zh, c, y, zl, x):
    return {"group": zh * 2 + c, "fsdp": y * 16 + zl * 4 + x}


def absolute_row(s, w, y, x):
    d, ab = lax.div(s, 2), lax.rem(s, 2)
    r, u = lax.div(w, 8), lax.rem(w, 8)
    near, zls = lax.div(u, 2), lax.rem(u, 2)
    far_y, near_x = lax.rem(y + d, 4), lax.rem(x + near, 4)
    far_x, near_y = lax.rem(x + d, 4), lax.rem(y + near, 4)
    row_a = far_y * 16 + zls * 4 + near_x
    row_b = near_y * 16 + (zls + 2) * 4 + far_x
    return jnp.where(ab == 0, row_a, row_b) * 3 + r


def kernel(
    tokens, gate_hbm, up_hbm, cot,
    hidden_out, token_out, gate_out, up_out,
    S, tokb, scr, X, Wp, gm, um, am_tx, am_rx, cotp, cotr, cotf,
    Pf, Ps, Pr, Q, Qs, Qr, Ac, Asc, H, TS, TO, RT, R1s, R1r, R2f, R2s, R2r, R3s, R3r, tscr,
    GG, UG,
    load_sem, out_sem, tx, rx,
):
    zh, c, y, zl, x = position()
    sib = place(zh, 1 - c, y, zl, x)
    anti = place(1 - zh, c, y, zl, x)
    antisib = place(1 - zh, 1 - c, y, zl, x)
    group_peers = (sib, anti, antisib)

    def at_x(d):
        return place(zh, c, y, zl, lax.rem(x + d, 4))

    def at_y(d):
        return place(zh, c, lax.rem(y + d, 4), zl, x)

    def at_z(d):
        return place(zh, c, y, lax.rem(zl + d, 4), x)

    used = [0]
    copies = []

    def send(src, dst, to):
        i = used[0]
        used[0] += 1
        cp = pltpu.make_async_remote_copy(
            src_ref=src, dst_ref=dst, send_sem=tx.at[i], recv_sem=rx.at[i],
            device_id=to, device_id_type=MESH,
        )
        cp.start()
        copies.append(cp)
        return cp

    loads = []
    for i in range(4):
        rows = pl.ds(i * 512, 512)
        for k, (src, dst) in enumerate(((gate_hbm, gm), (up_hbm, um))):
            cp = pltpu.make_async_copy(src.at[rows], dst.at[rows], load_sem.at[i, k])
            cp.start()
            loads.append(cp)
    barrier = pltpu.get_barrier_semaphore()
    peers = list(group_peers)
    for d in (1, 2, 3):
        peers += [at_x(d), at_y(d), at_z(d)]
    for p in peers:
        pl.semaphore_signal(barrier, inc=1, device_id=p, device_id_type=MESH)

    for j in range(64):
        tscr[pl.ds(j, 3, stride=64), :] = tokens[:, j * 128:(j + 1) * 128].astype(F32)
    for g in range(4):
        for r in range(3):
            tokb[g, r] = tscr[pl.ds(r * 64 + g * 16, 16), :].astype(BF16)

    q = lax.broadcasted_iota(jnp.int32, (192, 192), 0)
    col = lax.broadcasted_iota(jnp.int32, (192, 192), 1)
    pick = (col == absolute_row(lax.div(q, 24), lax.rem(q, 24), y, x)).astype(F32).astype(BF16)
    cperm = jnp.dot(pick, cot[...], preferred_element_type=F32)
    cotf[zh] = cperm
    cotp[...] = cperm.astype(BF16)

    tops = [jnp.zeros((8, FW), F32), jnp.zeros((8, FW), F32)]
    for i in range(4):
        for k, ref in enumerate((gm, um)):
            loads[2 * i + k].wait()

            def largest(b, top, ref=ref, i=i):
                v = jnp.abs(ref[pl.ds(i * 512 + b * 64, 64), :].astype(F32))
                return jnp.maximum(top, jnp.max(v.reshape(8, 8, FW), axis=0))

            tops[k] = lax.fori_loop(0, 8, largest, tops[k])
    for k in range(2):
        am_tx[0, pl.ds(8 * k, 8), :] = jnp.broadcast_to(
            jnp.max(tops[k], axis=(0, 1), keepdims=True), (8, 128)
        )

    pl.semaphore_wait(barrier, len(peers))

    gi = c * 2 + zh
    near = S.at[lax.div(zl, 2), 0, lax.rem(zl, 2)]
    s0 = []
    for p, (pz, pc) in zip(group_peers, ((zh, 1 - c), (1 - zh, c), (1 - zh, 1 - c))):
        s0.append(send(tokb.at[pz * 2 + pc], near.at[gi], p))
    near[gi] = tokb[zh * 2 + c]

    def share(stage, to):
        return [send(am_tx.at[stage], am_rx.at[3 * stage + i], p) for i, p in enumerate(to)]

    def merge(stage, cps):
        v = am_tx[stage]
        for i, cp in enumerate(cps):
            cp.wait_recv()
            v = jnp.maximum(v, am_rx[3 * stage + i])
        am_tx[stage + 1] = v

    m0 = share(0, group_peers)
    for cp in s0:
        cp.wait_recv()
    s1 = [send(near, near, at_z(d)) for d in (1, 2, 3)]
    merge(0, m0)
    m1 = share(1, [at_x(d) for d in (1, 2, 3)])
    merge(1, m1)
    m2 = share(2, [at_y(d) for d in (1, 2, 3)])
    for cp in s1:
        cp.wait_recv()
    s2 = [[], []]
    for d in (1, 3, 2):
        s2[0].append(send(S.at[0, 0], S.at[0, d], at_x(4 - d)))
        s2[1].append(send(S.at[1, 0], S.at[1, d], at_y(4 - d)))
    merge(2, m2)
    m3 = share(3, [at_z(d) for d in (1, 2, 3)])
    merge(3, m3)
    cot_copy = send(cotp, cotr, anti)

    g_amax = jnp.max(am_tx[4, 0:8, :], axis=(0, 1), keepdims=True)
    u_amax = jnp.max(am_tx[4, 8:16, :], axis=(0, 1), keepdims=True)
    g_factor, u_factor = QMAX / (g_amax + EPS), QMAX / (u_amax + EPS)
    g_scale, u_scale = (g_amax + EPS) / QMAX, (u_amax + EPS) / QMAX

    @pl.loop(0, 32)
    def _(b):
        rows = pl.ds(pl.multiple_of(b * 64, 64), 64)
        wg = jnp.floor(gm[rows, :].astype(F32) * g_factor + 0.5)
        wu = jnp.floor(um[rows, :].astype(F32) * u_factor + 0.5)
        Wp[rows, 0:FA] = wg[:, :FA].astype(BF16)
        Wp[rows, FA:2 * FA] = wu[:, :FA].astype(BF16)
        tail = jnp.concatenate([wg[:, FA:], wu[:, FA:], jnp.zeros((64, 64), F32)], axis=1)
        Wp[rows, 2 * FA:FP] = tail.astype(BF16)

    big = {1: [], 2: [], 3: []}

    def far(ab):
        return at_y if ab == 0 else at_x

    for ab in range(2):
        for cp in s2[ab]:
            cp.wait_recv()
        scr[ab] = S[ab].reshape(1536, 128).astype(F32)
        for k in range(0, 12, 2):
            for fb in range(16):
                lo = scr[ab, pl.ds(k * 16 + fb, 8, stride=192), :]
                hi = scr[ab, pl.ds((k + 1) * 16 + fb, 8, stride=192), :]
                X[ab, 8 * k:8 * k + 16, fb * 128:(fb + 1) * 128] = jnp.concatenate(
                    [lo, hi], axis=0
                ).astype(BF16)
        for d in ORDER:
            big[d].append(send(X.at[ab], X.at[2 * d + ab], far(ab)(4 - d)))

    p_copies, q_copies, a_copies = {}, {}, {}

    def forward(d):
        xs = X[2 * d:2 * d + 2].reshape(192, DQ)
        for n in range(0, FP, 256):
            width = min(256, FP - n)
            part = jnp.dot(xs, Wp[:, n:n + width], preferred_element_type=F32)
            Pf[d, :, :, n:n + width] = part.reshape(4, 48, width)
        for ab in range(2):
            Ps[d, ab] = Pf[d, 2 * ab + 1 - c].astype(BF16)
            p_copies[d, ab] = send(Ps.at[d, ab], Pr.at[d, ab], sib)

    def chip_sum(d, ab):
        p_copies[d, ab].wait_recv()
        v = Pf[d, 2 * ab + c] + Pr[d, ab].astype(F32)
        Q[d, ab] = v
        Qs[d, ab] = v.astype(BF16)

    def cross(d, ab):
        q_copies[d, ab] = send(Qs.at[d, ab], Qr.at[d, ab], anti)

    def act(d, ab):
        q_copies[d, ab].wait_recv()
        s = 2 * d + ab
        pre = Q[d, ab] + Qr[d, ab].astype(F32)
        gate = jnp.concatenate([pre[:, :FA], pre[:, 2 * FA:2 * FA + FT]], axis=1) * g_scale
        up = jnp.concatenate([pre[:, FA:2 * FA], pre[:, 2 * FA + FT:2 * FA + 2 * FT]], axis=1) * u_scale
        cotangent = cotf[:, s * 24:s * 24 + 24, :].reshape(48, FW)
        sig = jax.nn.sigmoid(gate)
        silu = gate * sig
        H[s * 48:s * 48 + 48, :] = (silu * up).astype(BF16)
        ga = cotangent * up * sig * (1.0 + gate * (1.0 - sig))
        ua = cotangent * silu
        packed = jnp.concatenate(
            [ga[:, :FA], ua[:, :FA], ga[:, FA:], ua[:, FA:], jnp.zeros((48, 64), F32)], axis=1
        )
        Ac[s, c] = packed.astype(BF16)
        a_copies[d, ab] = send(Ac.at[s, c], Ac.at[s, c], sib)

    lane = lax.broadcasted_iota(jnp.int32, (1, FP), 1)
    is_gate = (lane < FA) | ((lane >= 2 * FA) & (lane < 2 * FA + FT))
    scale_row = jnp.where(is_gate, g_scale, u_scale)

    def backward(d):
        for ab in range(2):
            a_copies[d, ab].wait_recv()
        Asc[...] = (Ac[2 * d:2 * d + 2].reshape(192, FP).astype(F32) * scale_row).astype(BF16)

        @pl.loop(0, 8)
        def _(j):
            cols = pl.ds(pl.multiple_of(j * 256, 256), 256)
            part = lax.dot_general(
                Asc[...], Wp[cols, :], (((1,), (1,)), ((), ())), preferred_element_type=F32
            )
            if d == 0:
                TO[:, cols] = part
            else:
                TS[d - 1, :, cols] = part.astype(BF16)

    rs = [[], []]

    def scatter(d):
        for ab in range(2):
            rs[ab].append(send(TS.at[d - 1, pl.ds(ab * 96, 96)], RT.at[d - 1, ab], far(ab)(d)))

    forward(0)
    chip_sum(0, 0)
    cross(0, 0)
    chip_sum(0, 1)
    for i, d in enumerate(ORDER):
        for cp in big[d]:
            cp.wait_recv()
        forward(d)
        for ab in range(2):
            chip_sum(d, ab)
            cross(d, ab)
        if i == 1:
            cot_copy.wait_recv()
            cotf[1 - zh] = cotr[...].astype(F32)
            act(0, 0)
    cross(0, 1)
    for d in ORDER:
        for ab in range(2):
            act(d, ab)
        backward(d)
        scatter(d)
    act(0, 1)
    backward(0)

    row = lax.broadcasted_iota(jnp.int32, (192, 384), 0)
    q = lax.broadcasted_iota(jnp.int32, (192, 384), 1)
    s, w = lax.div(q, 48), lax.rem(q, 48)
    mine = lax.div(w, 24) == zh
    pick = (mine & (row == absolute_row(s, lax.rem(w, 24), y, x))).astype(F32).astype(BF16)
    hidden_out[...] = jnp.dot(pick, H[...], preferred_element_type=F32).astype(BF16)

    def weight_grads(first, last):
        @pl.loop(first, last)
        def _(j):
            rows = pl.ds(pl.multiple_of(j * 256, 256), 256)
            part = lax.dot_general(
                X[:, :, rows].reshape(768, 256), Ac[...].reshape(768, FP),
                (((0,), (0,)), ((), ())), preferred_element_type=F32,
            )
            GG[rows, :] = jnp.concatenate(
                [part[:, :FA], part[:, 2 * FA:2 * FA + FT]], axis=1
            ).astype(BF16)
            UG[rows, :] = jnp.concatenate(
                [part[:, FA:2 * FA], part[:, 2 * FA + FT:2 * FA + 2 * FT]], axis=1
            ).astype(BF16)
            pltpu.make_async_copy(GG.at[rows], gate_out.at[rows], out_sem.at[j, 0]).start()
            pltpu.make_async_copy(UG.at[rows], up_out.at[rows], out_sem.at[j, 1]).start()

    weight_grads(0, 2)

    r1 = [[], []]
    for ab in range(2):
        for cp in rs[ab]:
            cp.wait_recv()
        for fb in range(16):
            cols = slice(fb * 128, (fb + 1) * 128)
            v = TO[ab * 96:ab * 96 + 96, cols]
            for i in range(3):
                v = v + RT[i, ab, :, cols].astype(F32)
            for k in range(12):
                scr[ab, pl.ds(k * 16 + fb, 8, stride=192), :] = v[8 * k:8 * k + 8]
        R1s[ab] = scr[ab].astype(BF16).reshape(4, 2, 4, 3, 16, 128)
        near_at = at_x if ab == 0 else at_y
        for d in (1, 3, 2):
            r1[ab].append(send(R1s.at[ab, d], R1r.at[ab, d - 1], near_at(d)))
    weight_grads(2, 4)
    for ab in range(2):
        for cp in r1[ab]:
            cp.wait_recv()
        v = scr[ab, 0:384, :]
        for i in range(3):
            v = v + R1r[ab, i].reshape(384, 128).astype(F32)
        R2f[2 * ab:2 * ab + 2] = v.reshape(2, 192, 128)
        R2s[2 * ab:2 * ab + 2] = v.astype(BF16).reshape(2, 4, 3, 16, 128)
    r2 = [send(R2s.at[lax.rem(zl + d, 4)], R2r.at[d - 1], at_z(d)) for d in (1, 2, 3)]
    weight_grads(4, 6)
    v = R2f[zl]
    for i, cp in enumerate(r2):
        cp.wait_recv()
        v = v + R2r[i].reshape(192, 128).astype(F32)
    R2f[zl] = v
    R3s[...] = v.astype(BF16).reshape(4, 3, 16, 128)
    r3 = []
    for i, (pz, pc) in enumerate(((zh, 1 - c), (1 - zh, c), (1 - zh, 1 - c))):
        r3.append(send(R3s.at[pc * 2 + pz], R3r.at[i], group_peers[i]))
    weight_grads(6, 8)
    for r in range(3):
        at = pl.ds(pl.multiple_of(r * 64 + (zh * 2 + c) * 16, 16), 16)
        tscr[at, :] = R2f[zl, pl.ds(pl.multiple_of(gi * 48 + r * 16, 16), 16), :]
    for i, (pz, pc) in enumerate(((zh, 1 - c), (1 - zh, c), (1 - zh, 1 - c))):
        r3[i].wait_recv()
        for r in range(3):
            at = pl.ds(pl.multiple_of(r * 64 + (pz * 2 + pc) * 16, 16), 16)
            tscr[at, :] = R3r[i, r].astype(F32)
    for j in range(64):
        token_out[:, j * 128:(j + 1) * 128] = tscr[pl.ds(j, 3, stride=64), :].astype(BF16)

    for cp in copies:
        cp.wait_send()

    @pl.loop(0, 8)
    def _(j):
        rows = pl.ds(pl.multiple_of(j * 256, 256), 256)
        pltpu.make_async_copy(GG.at[rows], gate_out.at[rows], out_sem.at[j, 0]).wait()
        pltpu.make_async_copy(UG.at[rows], up_out.at[rows], out_sem.at[j, 1]).wait()


def on_device(tokens, gate_master, up_master, hidden_cotangent):
    vmem = pl.BlockSpec(memory_space=pltpu.VMEM)
    anywhere = pl.BlockSpec(memory_space=pl.ANY)
    V = pltpu.VMEM
    n_copies = 96
    return pl.pallas_call(
        kernel,
        out_shape=(
            jax.ShapeDtypeStruct((192, FW), BF16),
            jax.ShapeDtypeStruct((3, 8192), BF16),
            jax.ShapeDtypeStruct((DQ, FW), BF16),
            jax.ShapeDtypeStruct((DQ, FW), BF16),
        ),
        in_specs=[vmem, anywhere, anywhere, vmem],
        out_specs=(vmem, vmem, anywhere, anywhere),
        scratch_shapes=[
            V((2, 4, 2, 4, 3, 16, 128), BF16),
            V((4, 3, 16, 128), BF16),
            V((2, 1536, 128), F32),
            V((8, 96, DQ), BF16),
            V((DQ, FP), BF16),
            V((DQ, FW), BF16),
            V((DQ, FW), BF16),
            V((5, 16, 128), F32),
            V((12, 16, 128), F32),
            V((192, FW), BF16),
            V((192, FW), BF16),
            V((2, 192, FW), F32),
            V((4, 4, 48, FP), F32),
            V((4, 2, 48, FP), BF16),
            V((4, 2, 48, FP), BF16),
            V((4, 2, 48, FP), F32),
            V((4, 2, 48, FP), BF16),
            V((4, 2, 48, FP), BF16),
            V((8, 2, 48, FP), BF16),
            V((192, FP), BF16),
            V((384, FW), BF16),
            V((3, 192, DQ), BF16),
            V((192, DQ), F32),
            V((3, 2, 96, DQ), BF16),
            V((2, 4, 2, 4, 3, 16, 128), BF16),
            V((2, 3, 2, 4, 3, 16, 128), BF16),
            V((4, 192, 128), F32),
            V((4, 4, 3, 16, 128), BF16),
            V((3, 4, 3, 16, 128), BF16),
            V((4, 3, 16, 128), BF16),
            V((3, 3, 16, 128), BF16),
            V((192, 128), F32),
            V((DQ, FW), BF16),
            V((DQ, FW), BF16),
            pltpu.SemaphoreType.DMA((4, 2)),
            pltpu.SemaphoreType.DMA((8, 2)),
            pltpu.SemaphoreType.DMA((n_copies,)),
            pltpu.SemaphoreType.DMA((n_copies,)),
        ],
        compiler_params=pltpu.CompilerParams(
            collective_id=0, has_side_effects=True, vmem_limit_bytes=58 * 2**20
        ),
        name="swiglu_step",
    )(tokens, gate_master, up_master, hidden_cotangent)


def solution(mesh):
    placed = (
        P(("group", "fsdp"), None),
        P("group", "fsdp"),
        P("group", "fsdp"),
        P("group", "fsdp"),
    )
    return jax.shard_map(
        on_device,
        mesh=mesh,
        in_specs=placed,
        out_specs=(
            P("group", "fsdp"),
            P(("group", "fsdp"), None),
            P("group", "fsdp"),
            P("group", "fsdp"),
        ),
        check_vma=False,
    )
```

time: 1090 us -> 125 us (0.11)
  the two profiles are of different devices: /device:TPU:0 before, /device:TPU:15 now
where the time goes in v1:
time: 125 us
  Pallas kernels  110 us (88%)
  local copies, waits for them, and re-layouts  13.8 us (11%)
    pallas_call x1, Pallas kernels, on_device(): pl.pallas_call(kernel, out_shape=(jax.ShapeDtypeStruct((192, FW), BF16),...  110 us
    unnamed x12, local copies, waits for them, and re-layouts  7.63 us
    pallas_call x2, local copies, waits for them, and re-layouts, on_device(): pl.pallas_call(kernel, out_shape=(jax.ShapeDtypeStruct((192, FW), BF16),...  6.22 us

profile of v1, /device:TPU:15, one launch (start us, length us, event | category | flops | bytes accessed | tf_op | source)
XLA Modules:
  0.0 124.6 jit_solution(13422136232007059747)
XLA Ops:
  0.6 0.0 copy-start.1
  0.6 3.9 %copy.8.gate_hbm = bf16[2048,416]{1,0:T(8,128)(2,1)} copy(bf16[2048,416]{0,1:T(8,128)(2,1)} %param.5) | data formatting | bytes 3407872 | tf_op args[1]
  4.5 0.0 copy-done.1
  4.5 2.4 %copy.9.up_hbm = bf16[2048,416]{1,0:T(8,128)(2,1)} copy(bf16[2048,416]{0,1:T(8,128)(2,1)S(1)} %copy-done.1) | data formatting | bytes 3407872 | tf_op args[2]
  6.9 110.1 %swiglu_step.1 = (bf16[192,416]{1,0:T(8,128)(2,1)}, bf16[3,8192]{1,0:T(4,128)(2,1)}, bf16[2048,416]{1,0:T(8,128)(2,1)}, bf16[2048,416]{1,0:T(8,128)(2,1)}) custom-call(bf16[3,8192]{1,0:T(4,128)(2,1)} %tokens.1, bf16[2048,416]{1,0:T(8,128)(2,1)} %copy.8.gate_hbm, bf16[2048,416]{1,0:T(8,128)(2,1)} %copy.9.up_hbm, bf16[192,416]{1,0:T(8,128)(2,1)} %cot.1), custom_call_target="tpu_custom_call" | custom-call | tf_op jit(solution)/shard_map/swiglu_step/pallas_call | solution.py:373
  117.1 0.0 copy-start
  117.1 4.0 %copy.10 = bf16[2048,416]{0,1:T(8,128)(2,1)} copy(bf16[2048,416]{1,0:T(8,128)(2,1)} %get-tuple-element.6) | data formatting | bytes 3407872 | tf_op jit(solution)/shard_map/swiglu_step/pallas_call | solution.py:373
  121.1 0.0 copy-done
  121.1 0.0 copy-start.2
  121.1 0.0 copy-start.3
  121.1 2.2 %copy.11 = bf16[2048,416]{0,1:T(8,128)(2,1)} copy(bf16[2048,416]{1,0:T(8,128)(2,1)S(1)} %copy-done) | data formatting | bytes 3407872 | tf_op jit(solution)/shard_map/swiglu_step/pallas_call | solution.py:373
  123.3 0.0 copy-done.2
  123.3 0.7 copy.14
  124.0 0.0 copy-done.3
  124.0 0.6 copy.15
Async XLA Ops:
  0.6 3.9 %copy-start.1 = (bf16[2048,416]{0,1:T(8,128)(2,1)S(1)}, bf16[2048,416]{0,1:T(8,128)(2,1)}, u32[]{:S(2)}) copy-start(bf16[2048,416]{0,1:T(8,128)(2,1)} %param.6) | copy-start | bytes 5111812
  117.1 4.0 %copy-start = (bf16[2048,416]{1,0:T(8,128)(2,1)S(1)}, bf16[2048,416]{1,0:T(8,128)(2,1)}, u32[]{:S(2)}) copy-start(bf16[2048,416]{1,0:T(8,128)(2,1)} %get-tuple-element.7) | copy-start | bytes 5111812
  121.1 2.3 %copy-start.2 = (bf16[192,416]{1,0:T(8,128)(2,1)S(1)}, bf16[192,416]{1,0:T(8,128)(2,1)}, u32[]{:S(2)}) copy-start(bf16[192,416]{1,0:T(8,128)(2,1)} %get-tuple-element.12) | copy-start | bytes 479236
  121.1 2.9 %copy-start.3 = (bf16[3,8192]{1,0:T(4,128)(2,1)S(1)}, bf16[3,8192]{1,0:T(4,128)(2,1)}, u32[]{:S(2)}) copy-start(bf16[3,8192]{1,0:T(4,128)(2,1)} %get-tuple-element.13) | copy-start | bytes 147460

commit v2 on v0

v2 whole, which is shorter than its diff:
```python
import functools

import jax
import jax.numpy as jnp
from jax import lax
from jax.experimental import pallas as pl
from jax.experimental.pallas import tpu as pltpu
from jax.sharding import PartitionSpec as P

QMAX = 60.0
EPS = 1e-06
MESH = pl.DeviceIdType.MESH
F32 = jnp.float32
BF16 = jnp.bfloat16

DQ = 2048
FW = 416
FA = 384
FT = FW - FA
FP = 2 * FW
SEAT = tuple((k % 2) * 6 + (k // 2 % 2) * 3 + k // 4 for k in range(12))
LOADS = ((0, 112), (112, 112), (224, 96), (320, 96))
FAR = (1, 3, 2)


def position():
    g = lax.axis_index("group")
    f = lax.axis_index("fsdp")
    return lax.div(g, 2), lax.rem(g, 2), lax.div(f, 16), lax.rem(lax.div(f, 4), 4), lax.rem(f, 4)


def place(zh, c, y, zl, x):
    return {"group": zh * 2 + c, "fsdp": y * 16 + zl * 4 + x}


def absolute_row(n, y, x):
    chunk, i, u = lax.div(n, 48), lax.div(lax.rem(n, 48), 8), lax.rem(n, 8)
    ab, three = lax.div(i, 3), lax.rem(i, 3)
    near, zls = lax.div(u, 2), lax.rem(u, 2)
    d = jnp.where(chunk == 0, 0, jnp.where(three == 0, FAR[0], jnp.where(three == 1, FAR[1], FAR[2])))
    r = jnp.where(chunk == 0, three, chunk - 1)
    row_a = lax.rem(y + d, 4) * 16 + zls * 4 + lax.rem(x + near, 4)
    row_b = lax.rem(y + near, 4) * 16 + (zls + 2) * 4 + lax.rem(x + d, 4)
    return jnp.where(ab == 0, row_a, row_b) * 3 + r


def kernel(
    tokens, gate_hbm, up_hbm, cot,
    hidden_out, token_out, gate_out, up_out,
    S, tokb, TK, scr, X, Wt, gm, um, am_tx, am_rx, cotf,
    Pf, Ps, Pr, Qs, Qr, Ag, Ax, Asc, H, TS, TO, RT, scr2, R1s, R1r, R2f, R2s, R2r, acc, R3s, R3r, R3f, tscr,
    At, GG, UG,
    load_sem, out_sem, tx, rx,
):
    zh, c, y, zl, x = position()
    sib = place(zh, 1 - c, y, zl, x)
    anti = place(1 - zh, c, y, zl, x)
    z = zh * 4 + zl

    def at_x(d):
        return place(zh, c, y, zl, lax.rem(x + d, 4))

    def at_y(d):
        return place(zh, c, lax.rem(y + d, 4), zl, x)

    def at_z(d):
        to = lax.rem(z + d, 8)
        return place(lax.div(to, 4), c, y, lax.rem(to, 4), x)

    xs_to, ys_to = [at_x(d) for d in (1, 2, 3)], [at_y(d) for d in (1, 2, 3)]
    zs_to = [at_z(d) for d in range(1, 8)]

    used = [0]
    copies = []

    def send(src, dst, to):
        i = used[0]
        used[0] += 1
        cp = pltpu.make_async_remote_copy(
            src_ref=src, dst_ref=dst, send_sem=tx.at[i], recv_sem=rx.at[i],
            device_id=to, device_id_type=MESH,
        )
        cp.start()
        copies.append(cp)
        return cp

    loads = []
    for i, (start, count) in enumerate(LOADS):
        rows = pl.ds(start, count)
        for k, (src, dst) in enumerate(((gate_hbm, gm), (up_hbm, um))):
            cp = pltpu.make_async_copy(src.at[rows], dst.at[rows], load_sem.at[i, k])
            cp.start()
            loads.append(cp)
    barrier = pltpu.get_barrier_semaphore()
    peers = [sib] + xs_to + ys_to + zs_to
    for p in peers:
        pl.semaphore_signal(barrier, inc=1, device_id=p, device_id_type=MESH)

    for j in range(64):
        tscr[pl.ds(j, 3, stride=64), :] = tokens[:, j * 128:(j + 1) * 128].astype(F32)
    for g in range(4):
        for r in range(3):
            tokb[g % 2, g // 2, r] = tscr[pl.ds(r * 64 + g * 16, 16), :].astype(BF16)

    pl.semaphore_wait(barrier, len(peers))

    t0 = send(tokb.at[1 - c], TK.at[:, c], sib)
    TK[:, c] = tokb[c]

    tops = [jnp.zeros((16, DQ), BF16), jnp.zeros((16, DQ), BF16)]
    for i, (start, count) in enumerate(LOADS):
        for k, ref in enumerate((gm, um)):
            loads[2 * i + k].wait()

            def largest(b, top, ref=ref, start=start):
                rows = pl.ds(pl.multiple_of(start + b * 16, 16), 16)
                return jnp.maximum(top, jnp.abs(ref[rows, :]))

            tops[k] = lax.fori_loop(0, count // 16, largest, tops[k])
    for k in range(2):
        am_tx[0, pl.ds(8 * k, 8), :] = jnp.broadcast_to(
            jnp.max(tops[k].astype(F32), axis=(0, 1), keepdims=True), (8, 128)
        )

    def share(stage, first, to):
        return [send(am_tx.at[stage], am_rx.at[first + i], p) for i, p in enumerate(to)]

    def merge(stage, first, cps):
        v = am_tx[stage]
        for i, cp in enumerate(cps):
            cp.wait_recv()
            v = jnp.maximum(v, am_rx[first + i])
        am_tx[stage + 1] = v

    m = share(0, 0, [sib])
    t0.wait_recv()
    near = S.at[lax.div(zl, 2), 0, lax.rem(zl, 2), zh]
    t1 = []
    for d, p in enumerate(zs_to):
        t1.append(send(TK.at[lax.div(lax.rem(z + d + 1, 8), 4)], near, p))
    near[...] = TK[zh]
    merge(0, 0, m)
    m = share(1, 1, xs_to)

    mine = absolute_row(lax.broadcasted_iota(jnp.int32, (192, 1), 0), y, x)
    col = lax.broadcasted_iota(jnp.int32, (192, 192), 1)
    pick = (col == mine).astype(F32).astype(BF16)
    cotf[...] = jnp.dot(pick, cot[...], preferred_element_type=F32)
    merge(1, 1, m)
    m = share(2, 4, ys_to)
    merge(2, 4, m)
    m = share(3, 7, zs_to)
    for cp in t1:
        cp.wait_recv()
    s2 = [[], []]
    for d in (1, 3, 2):
        s2[0].append(send(S.at[0, 0], S.at[0, d], at_x(4 - d)))
        s2[1].append(send(S.at[1, 0], S.at[1, d], at_y(4 - d)))
    merge(3, 7, m)

    g_amax = jnp.max(am_tx[4, 0:8, :], axis=(0, 1), keepdims=True)
    u_amax = jnp.max(am_tx[4, 8:16, :], axis=(0, 1), keepdims=True)
    g_factor, u_factor = QMAX / (g_amax + EPS), QMAX / (u_amax + EPS)
    g_scale, u_scale = (g_amax + EPS) / QMAX, (u_amax + EPS) / QMAX

    def quantized(ref, rows, factor):
        return jnp.floor(ref[rows, :].astype(F32) * factor + 0.5).astype(BF16)

    @pl.loop(0, FA // 16)
    def _(b):
        rows = pl.ds(pl.multiple_of(b * 16, 16), 16)
        Wt[rows, :] = quantized(gm, rows, g_factor)
        Wt[pl.ds(pl.multiple_of(FA + b * 16, 16), 16), :] = quantized(um, rows, u_factor)

    for t in range(0, FT, 16):
        Wt[2 * FA + t:2 * FA + t + 16, :] = quantized(gm, pl.ds(FA + t, 16), g_factor)
        Wt[2 * FA + FT + t:2 * FA + FT + t + 16, :] = quantized(um, pl.ds(FA + t, 16), u_factor)

    def far(ab):
        return at_y if ab == 0 else at_x

    for ab in range(2):
        for cp in s2[ab]:
            cp.wait_recv()
        scr[ab] = S[ab].reshape(1536, 128).astype(F32)
        for k in range(0, 12, 2):
            for fb in range(16):
                lo = scr[ab, pl.ds(SEAT[k] * 16 + fb, 8, stride=192), :]
                hi = scr[ab, pl.ds(SEAT[k + 1] * 16 + fb, 8, stride=192), :]
                at = ab * 96 + 8 * k
                X[0, at:at + 16, fb * 128:(fb + 1) * 128] = jnp.concatenate([lo, hi], axis=0).astype(BF16)

    big = {}

    def gather(q):
        big[q] = []
        for t, d in enumerate(FAR):
            for ab in range(2):
                own = pl.ds(ab * 96 + (q - 1) * 32, 32)
                there = pl.ds((ab * 3 + t) * 32, 32)
                big[q].append(send(X.at[0, own], X.at[q, there], far(ab)(4 - d)))

    p_copies, q_copies, sib_copies, anti_copies, fwd_copies = {}, {}, {}, {}, {}

    def forward(q):
        for n in range(0, FP, 256):
            width = min(256, FP - n)
            part = lax.dot_general(
                X[q], Wt[n:n + width, :], (((1,), (1,)), ((), ())), preferred_element_type=F32
            )
            for i in range(6):
                for k in range(4):
                    at = (i * 4 + k) * 8
                    Pf[q, k // 2, k % 2, i * 8:i * 8 + 8, n:n + width] = part[at:at + 8]
        Ps[q] = Pf[q, 1 - c].astype(BF16)
        p_copies[q] = send(Ps.at[q], Pr.at[q], sib)

    def cross(q):
        p_copies[q].wait_recv()
        Qs[q] = (Pf[q, c, 1 - zh] + Pr[q, 1 - zh].astype(F32)).astype(BF16)
        q_copies[q] = send(Qs.at[q], Qr.at[q], anti)

    def act(q):
        own = Pf[q, c, zh] + Pr[q, zh].astype(F32)
        q_copies[q].wait_recv()
        pre = own + Qr[q].astype(F32)
        gate = jnp.concatenate([pre[:, :FA], pre[:, 2 * FA:2 * FA + FT]], axis=1) * g_scale
        up = jnp.concatenate([pre[:, FA:2 * FA], pre[:, 2 * FA + FT:FP]], axis=1) * u_scale
        cotangent = cotf[q * 48:q * 48 + 48, :]
        sig = jax.nn.sigmoid(gate)
        silu = gate * sig
        H[q * 48:q * 48 + 48, :] = (silu * up).astype(BF16)
        ga = cotangent * up * sig * (1.0 + gate * (1.0 - sig))
        ua = cotangent * silu
        packed = jnp.concatenate([ga[:, :FA], ua[:, :FA], ga[:, FA:], ua[:, FA:]], axis=1)
        Ag[q, c, zh] = packed.astype(BF16)
        sib_copies[q] = send(Ag.at[q, c, zh], Ag.at[q, c, zh], sib)

    def cross_back(q):
        anti_copies[q] = send(Ag.at[q, c, zh], Ag.at[q, c, zh], anti)

    def pass_on(q):
        anti_copies[q].wait_recv()
        fwd_copies[q] = send(Ag.at[q, c, 1 - zh], Ag.at[q, c, 1 - zh], sib)

    lane = lax.broadcasted_iota(jnp.int32, (1, FP), 1)
    is_gate = (lane < FA) | ((lane >= 2 * FA) & (lane < 2 * FA + FT))
    scale_row = jnp.where(is_gate, g_scale, u_scale)
    rs = {}

    def backward(q):
        sib_copies[q].wait_recv()
        fwd_copies[q].wait_recv()
        parts = [Ag[q, k // 2, k % 2].astype(F32) for k in range(4)]
        rows = jnp.concatenate(
            [parts[k][i * 8:i * 8 + 8] for i in range(6) for k in range(4)], axis=0
        )
        Ax[q] = rows.astype(BF16)
        Asc[...] = (rows * scale_row).astype(BF16)
        for f in range(2):

            @pl.loop(0, 4)
            def _(j):
                cols = pl.ds(pl.multiple_of(j * 256, 256), 256)
                from_ = pl.ds(pl.multiple_of(f * 1024 + j * 256, 256), 256)
                part = jnp.dot(Asc[...], Wt[:, from_], preferred_element_type=F32)
                if q == 0:
                    TO[f, :, cols] = part
                else:
                    TS[q - 1, f, :, cols] = part.astype(BF16)

            if q == 3:
                scatter(q, f)
        if q in (1, 2):
            scatter(q, None)

    def scatter(q, f):
        fs = slice(None) if f is None else f
        rs[q, f] = []
        for t, d in enumerate(FAR):
            for ab in range(2):
                here = pl.ds((ab * 3 + t) * 32, 32)
                there = pl.ds((q - 1) * 32, 32)
                rs[q, f].append(
                    send(TS.at[q - 1, fs, here], RT.at[fs, ab, d - 1, there], far(ab)(d))
                )

    gather(1)
    forward(0)
    gather(2)
    cross(0)
    for cp in big[1]:
        cp.wait_recv()
    forward(1)
    gather(3)
    cross(1)
    act(0)
    for cp in big[2]:
        cp.wait_recv()
    forward(2)
    cross(2)
    act(1)
    cross_back(1)
    for cp in big[3]:
        cp.wait_recv()
    forward(3)
    cross(3)
    act(2)
    cross_back(2)
    pass_on(1)
    backward(1)
    act(3)
    cross_back(3)
    cross_back(0)
    pass_on(2)
    backward(2)
    pass_on(3)
    backward(3)
    pass_on(0)
    backward(0)

    row = lax.broadcasted_iota(jnp.int32, (192, 192), 0)
    mine = absolute_row(lax.broadcasted_iota(jnp.int32, (1, 192), 1), y, x)
    pick = (row == mine).astype(F32).astype(BF16)
    hidden_out[...] = jnp.dot(pick, H[...], preferred_element_type=F32).astype(BF16)

    for i in range(6):
        At[:, i * 128:(i + 1) * 128] = Ax[...].reshape(768, FP)[i * 128:(i + 1) * 128, :].T

    def weight_grads(first, last):
        @pl.loop(first, last)
        def _(j):
            cols = pl.ds(pl.multiple_of(j * 256, 256), 256)
            part = jnp.dot(
                At[...], X[:, :, cols].reshape(768, 256), preferred_element_type=F32
            ).astype(BF16)
            GG[0:FA, cols] = part[0:FA]
            GG[FA:FW, cols] = part[2 * FA:2 * FA + FT]
            UG[0:FA, cols] = part[FA:2 * FA]
            UG[FA:FW, cols] = part[2 * FA + FT:FP]
            pltpu.make_async_copy(GG.at[:, cols], gate_out.at[:, cols], out_sem.at[j, 0]).start()
            pltpu.make_async_copy(UG.at[:, cols], up_out.at[:, cols], out_sem.at[j, 1]).start()

    weight_grads(0, 3)

    def near_scatter(f):
        out = [[], []]
        for cp in rs[3, f]:
            cp.wait_recv()
        for ab in range(2):
            for fb in range(8):
                cols = slice(fb * 128, (fb + 1) * 128)
                v = TO[f, ab * 96:ab * 96 + 96, cols]
                for i in range(3):
                    v = v + RT[f, ab, i, :, cols].astype(F32)
                for k in range(12):
                    scr2[f, ab, pl.ds(SEAT[k] * 8 + fb, 8, stride=96), :] = v[8 * k:8 * k + 8]
            R1s[f, ab] = scr2[f, ab].astype(BF16).reshape(4, 192, 128)
            near_at = at_x if ab == 0 else at_y
            for d in FAR:
                out[ab].append(send(R1s.at[f, ab, d], R1r.at[f, ab, d - 1], near_at(d)))
        return out

    def column_scatter(f, r1):
        for ab in range(2):
            for cp in r1[ab]:
                cp.wait_recv()
            v = scr2[f, ab, 0:192, :]
            for i in range(3):
                v = v + R1r[f, ab, i].astype(F32)
            R2f[f, 2 * ab:2 * ab + 2] = v.reshape(2, 2, 48, 128)
            R2s[f, 2 * ab:2 * ab + 2] = v.astype(BF16).reshape(2, 2, 48, 128)
        out = []
        for d, p in enumerate(zs_to):
            to = lax.rem(z + d + 1, 8)
            out.append(send(R2s.at[f, lax.rem(to, 4), lax.div(to, 4)], R2r.at[f, d], p))
        return out

    def column_sum(f, r2):
        acc[f, zh] = R2f[f, zl, zh]
        acc[f, 1 - zh] = jnp.zeros((48, 128), F32)
        for d, cp in enumerate(r2):
            cp.wait_recv()
            half = lax.div(lax.rem(z + 7 - d, 8), 4)
            acc[f, half] = acc[f, half] + R2r[f, d].astype(F32)

    for q in (1, 2):
        for cp in rs[q, None]:
            cp.wait_recv()
    r1a = near_scatter(0)
    r1b = near_scatter(1)
    weight_grads(3, 4)
    r2a = column_scatter(0, r1a)
    r2b = column_scatter(1, r1b)
    weight_grads(4, 7)
    column_sum(0, r2a)
    column_sum(1, r2b)
    theirs = pl.ds(pl.multiple_of((1 - c) * 24, 8), 24)
    R3s[...] = jnp.concatenate(
        [acc[f, h, theirs, :] for h in range(2) for f in range(2)], axis=0
    ).astype(BF16)
    r3 = send(R3s, R3r, sib)
    weight_grads(7, 8)
    for h in range(2):
        for f in range(2):
            for r in range(3):
                at = pl.ds(pl.multiple_of(r * 64 + (h * 2 + c) * 16 + f * 8, 8), 8)
                tscr[at, :] = acc[f, h, pl.ds(pl.multiple_of(c * 24 + r * 8, 8), 8), :]
    r3.wait_recv()
    R3f[...] = R3r[...].astype(F32)
    for h in range(2):
        for f in range(2):
            for r in range(3):
                at = pl.ds(pl.multiple_of(r * 64 + (h * 2 + 1 - c) * 16 + f * 8, 8), 8)
                b = (h * 2 + f) * 24 + r * 8
                tscr[at, :] = R3f[b:b + 8, :]
    for j in range(64):
        token_out[:, j * 128:(j + 1) * 128] = tscr[pl.ds(j, 3, stride=64), :].astype(BF16)

    for cp in copies:
        cp.wait_send()

    @pl.loop(0, 8)
    def _(j):
        cols = pl.ds(pl.multiple_of(j * 256, 256), 256)
        pltpu.make_async_copy(GG.at[:, cols], gate_out.at[:, cols], out_sem.at[j, 0]).wait()
        pltpu.make_async_copy(UG.at[:, cols], up_out.at[:, cols], out_sem.at[j, 1]).wait()


def on_device(tokens, gate_master, up_master, hidden_cotangent):
    vmem = pl.BlockSpec(memory_space=pltpu.VMEM)
    anywhere = pl.BlockSpec(memory_space=pl.ANY)
    V = pltpu.VMEM
    n_copies = 128
    hidden, token_grad, gate_grad, up_grad = pl.pallas_call(
        kernel,
        out_shape=(
            jax.ShapeDtypeStruct((192, FW), BF16),
            jax.ShapeDtypeStruct((3, 8192), BF16),
            jax.ShapeDtypeStruct((FW, DQ), BF16),
            jax.ShapeDtypeStruct((FW, DQ), BF16),
        ),
        in_specs=[vmem, anywhere, anywhere, vmem],
        out_specs=(vmem, vmem, anywhere, anywhere),
        scratch_shapes=[
            V((2, 4, 2, 2, 2, 3, 16, 128), BF16),
            V((2, 2, 3, 16, 128), BF16),
            V((2, 2, 3, 16, 128), BF16),
            V((2, 1536, 128), F32),
            V((4, 192, DQ), BF16),
            V((FP, DQ), BF16),
            V((FW, DQ), BF16),
            V((FW, DQ), BF16),
            V((5, 16, 128), F32),
            V((14, 16, 128), F32),
            V((192, FW), F32),
            V((4, 2, 2, 48, FP), F32),
            V((4, 2, 48, FP), BF16),
            V((4, 2, 48, FP), BF16),
            V((4, 48, FP), BF16),
            V((4, 48, FP), BF16),
            V((4, 2, 2, 48, FP), BF16),
            V((4, 192, FP), BF16),
            V((192, FP), BF16),
            V((192, FW), BF16),
            V((3, 2, 192, 1024), BF16),
            V((2, 192, 1024), F32),
            V((2, 2, 3, 96, 1024), BF16),
            V((2, 2, 768, 128), F32),
            V((2, 2, 4, 192, 128), BF16),
            V((2, 2, 3, 192, 128), BF16),
            V((2, 4, 2, 48, 128), F32),
            V((2, 4, 2, 48, 128), BF16),
            V((2, 7, 48, 128), BF16),
            V((2, 2, 48, 128), F32),
            V((96, 128), BF16),
            V((96, 128), BF16),
            V((96, 128), F32),
            V((192, 128), F32),
            V((FP, 768), BF16),
            V((FW, DQ), BF16),
            V((FW, DQ), BF16),
            pltpu.SemaphoreType.DMA((4, 2)),
            pltpu.SemaphoreType.DMA((8, 2)),
            pltpu.SemaphoreType.DMA((n_copies,)),
            pltpu.SemaphoreType.DMA((n_copies,)),
        ],
        compiler_params=pltpu.CompilerParams(
            collective_id=0, has_side_effects=True, vmem_limit_bytes=58 * 2**20
        ),
        name="swiglu_step",
    )(tokens, gate_master.T, up_master.T, hidden_cotangent)
    return hidden, token_grad, gate_grad.T, up_grad.T


def solution(mesh):
    placed = (
        P(("group", "fsdp"), None),
        P("group", "fsdp"),
        P("group", "fsdp"),
        P("group", "fsdp"),
    )
    return jax.shard_map(
        on_device,
        mesh=mesh,
        in_specs=placed,
        out_specs=(
            P("group", "fsdp"),
            P(("group", "fsdp"), None),
            P("group", "fsdp"),
            P("group", "fsdp"),
        ),
        check_vma=False,
    )
```

time: 1090 us -> 104 us (0.10)
  the two profiles are of different devices: /device:TPU:0 before, /device:TPU:1 now
where the time goes in v2:
time: 104 us; the launch traced here: 103 us
  Pallas kernels  95.4 us (92%)
  local copies, waits for them, and re-layouts  7.26 us (7%)
    pallas_call x1, Pallas kernels, on_device(): pl.pallas_call(kernel, out_shape=(jax.ShapeDtypeStruct((192, FW), BF16),...  95.4 us
    unnamed x6, local copies, waits for them, and re-layouts  7.26 us

profile of v2, /device:TPU:1, one launch (start us, length us, event | category | flops | bytes accessed | tf_op | source)
XLA Modules:
  0.0 103.3 jit_solution(12440683676843740035)
XLA Ops:
  0.6 95.4 %swiglu_step.1 = (bf16[192,416]{1,0:T(8,128)(2,1)}, bf16[3,8192]{1,0:T(4,128)(2,1)}, bf16[416,2048]{1,0:T(8,128)(2,1)}, bf16[416,2048]{1,0:T(8,128)(2,1)}) custom-call(bf16[3,8192]{1,0:T(4,128)(2,1)} %tokens.1, bf16[416,2048]{1,0:T(8,128)(2,1)} %bitcast.4, bf16[416,2048]{1,0:T(8,128)(2,1)} %bitcast.5, bf16[192,416]{1,0:T(8,128)(2,1)} %cot.1), custom_call_target="tpu_custom_call" | custom-call | tf_op jit(solution)/shard_map/swiglu_step/pallas_call | solution.py:435
  96.1 1.6 %copy.12 = bf16[192,416]{1,0:T(8,128)(2,1)} copy(bf16[192,416]{1,0:T(8,128)(2,1)} %get-tuple-element.16) | data formatting | bytes 319488
  97.7 1.5 %copy.13 = bf16[3,8192]{1,0:T(4,128)(2,1)} copy(bf16[3,8192]{1,0:T(4,128)(2,1)} %get-tuple-element.17) | data formatting | bytes 98304
  99.2 0.0 copy-start
  99.2 3.0 %copy.14 = bf16[2048,416]{0,1:T(8,128)(2,1)} copy(bf16[2048,416]{0,1:T(8,128)(2,1)} %bitcast.7) | data formatting | bytes 3407872
  102.1 0.0 copy-done
  102.1 1.2 %copy.15 = bf16[2048,416]{0,1:T(8,128)(2,1)} copy(bf16[2048,416]{0,1:T(8,128)(2,1)S(1)} %bitcast.6) | data formatting | bytes 3407872
Async XLA Ops:
  99.2 3.0 %copy-start = (bf16[416,2048]{1,0:T(8,128)(2,1)S(1)}, bf16[416,2048]{1,0:T(8,128)(2,1)}, u32[]{:S(2)}) copy-start(bf16[416,2048]{1,0:T(8,128)(2,1)} %get-tuple-element.11) | copy-start | bytes 5111812

commit v3 on v2

--- a/solution.py
+++ b/solution.py
@@ -46,11 +46,11 @@
 
 def kernel(
     tokens, gate_hbm, up_hbm, cot,
-    hidden_out, token_out, gate_out, up_out,
+    hidden_out, token_out, GG, UG,
     S, tokb, TK, scr, X, Wt, gm, um, am_tx, am_rx, cotf,
-    Pf, Ps, Pr, Qs, Qr, Ag, Ax, Asc, H, TS, TO, RT, scr2, R1s, R1r, R2f, R2s, R2r, acc, R3s, R3r, R3f, tscr,
-    At, GG, UG,
-    load_sem, out_sem, tx, rx,
+    Pf, Ps, Pr, Qs, Qr, Ag, Ax, Asc, H, TS, TO, RT, scr2, R1s, R1r, R2f, R2s, R2r, acc, R3s, R3r, tscr,
+    At,
+    load_sem, tx, rx,
 ):
     zh, c, y, zl, x = position()
     sib = place(zh, 1 - c, y, zl, x)
@@ -102,11 +102,6 @@
         for r in range(3):
             tokb[g % 2, g // 2, r] = tscr[pl.ds(r * 64 + g * 16, 16), :].astype(BF16)
 
-    pl.semaphore_wait(barrier, len(peers))
-
-    t0 = send(tokb.at[1 - c], TK.at[:, c], sib)
-    TK[:, c] = tokb[c]
-
     tops = [jnp.zeros((16, DQ), BF16), jnp.zeros((16, DQ), BF16)]
     for i, (start, count) in enumerate(LOADS):
         for k, ref in enumerate((gm, um)):
@@ -121,6 +116,11 @@
         am_tx[0, pl.ds(8 * k, 8), :] = jnp.broadcast_to(
             jnp.max(tops[k].astype(F32), axis=(0, 1), keepdims=True), (8, 128)
         )
+
+    pl.semaphore_wait(barrier, len(peers))
+
+    t0 = send(tokb.at[1 - c], TK.at[:, c], sib)
+    TK[:, c] = tokb[c]
 
     def share(stage, first, to):
         return [send(am_tx.at[stage], am_rx.at[first + i], p) for i, p in enumerate(to)]
@@ -295,6 +295,7 @@
     gather(3)
     cross(1)
     act(0)
+    cross_back(0)
     for cp in big[2]:
         cp.wait_recv()
     forward(2)
@@ -305,27 +306,28 @@
         cp.wait_recv()
     forward(3)
     cross(3)
+    pass_on(0)
     act(2)
     cross_back(2)
+    backward(0)
     pass_on(1)
     backward(1)
     act(3)
     cross_back(3)
-    cross_back(0)
     pass_on(2)
     backward(2)
     pass_on(3)
     backward(3)
-    pass_on(0)
-    backward(0)
-
-    row = lax.broadcasted_iota(jnp.int32, (192, 192), 0)
-    mine = absolute_row(lax.broadcasted_iota(jnp.int32, (1, 192), 1), y, x)
-    pick = (row == mine).astype(F32).astype(BF16)
-    hidden_out[...] = jnp.dot(pick, H[...], preferred_element_type=F32).astype(BF16)
-
-    for i in range(6):
-        At[:, i * 128:(i + 1) * 128] = Ax[...].reshape(768, FP)[i * 128:(i + 1) * 128, :].T
+
+    def write_hidden():
+        row = lax.broadcasted_iota(jnp.int32, (192, 192), 0)
+        there = absolute_row(lax.broadcasted_iota(jnp.int32, (1, 192), 1), y, x)
+        pick = (row == there).astype(F32).astype(BF16)
+        hidden_out[...] = jnp.dot(pick, H[...], preferred_element_type=F32).astype(BF16)
+
+    def transpose_acts():
+        for i in range(6):
+            At[:, i * 128:(i + 1) * 128] = Ax[...].reshape(768, FP)[i * 128:(i + 1) * 128, :].T
 
     def weight_grads(first, last):
         @pl.loop(first, last)
@@ -338,110 +340,103 @@
             GG[FA:FW, cols] = part[2 * FA:2 * FA + FT]
             UG[0:FA, cols] = part[FA:2 * FA]
             UG[FA:FW, cols] = part[2 * FA + FT:FP]
-            pltpu.make_async_copy(GG.at[:, cols], gate_out.at[:, cols], out_sem.at[j, 0]).start()
-            pltpu.make_async_copy(UG.at[:, cols], up_out.at[:, cols], out_sem.at[j, 1]).start()
-
-    weight_grads(0, 3)
-
-    def near_scatter(f):
+
+    def near_scatter(r, arrived):
+        for cp in arrived:
+            cp.wait_recv()
         out = [[], []]
-        for cp in rs[3, f]:
-            cp.wait_recv()
+        there = slice(r * 32, r * 32 + 32)
         for ab in range(2):
-            for fb in range(8):
-                cols = slice(fb * 128, (fb + 1) * 128)
-                v = TO[f, ab * 96:ab * 96 + 96, cols]
-                for i in range(3):
-                    v = v + RT[f, ab, i, :, cols].astype(F32)
-                for k in range(12):
-                    scr2[f, ab, pl.ds(SEAT[k] * 8 + fb, 8, stride=96), :] = v[8 * k:8 * k + 8]
-            R1s[f, ab] = scr2[f, ab].astype(BF16).reshape(4, 192, 128)
+            for f in range(2):
+                for fb in range(8):
+                    cols = slice(fb * 128, (fb + 1) * 128)
+                    v = TO[f, ab * 96 + r * 32:ab * 96 + r * 32 + 32, cols]
+                    for i in range(3):
+                        v = v + RT[f, ab, i, there, cols].astype(F32)
+                    for k in range(4):
+                        seat = (k % 2) * 2 + k // 2
+                        at = pl.ds(seat * 16 + f * 8 + fb, 8, stride=64)
+                        scr2[r, ab, at, :] = v[8 * k:8 * k + 8]
+            R1s[r, ab] = scr2[r, ab].astype(BF16).reshape(4, 128, 128)
             near_at = at_x if ab == 0 else at_y
             for d in FAR:
-                out[ab].append(send(R1s.at[f, ab, d], R1r.at[f, ab, d - 1], near_at(d)))
+                out[ab].append(send(R1s.at[r, ab, d], R1r.at[r, ab, d - 1], near_at(d)))
         return out
 
-    def column_scatter(f, r1):
+    def column_scatter(r, r1):
         for ab in range(2):
             for cp in r1[ab]:
                 cp.wait_recv()
-            v = scr2[f, ab, 0:192, :]
+            v = scr2[r, ab, 0:128, :]
             for i in range(3):
-                v = v + R1r[f, ab, i].astype(F32)
-            R2f[f, 2 * ab:2 * ab + 2] = v.reshape(2, 2, 48, 128)
-            R2s[f, 2 * ab:2 * ab + 2] = v.astype(BF16).reshape(2, 2, 48, 128)
+                v = v + R1r[r, ab, i].astype(F32)
+            R2f[r, 2 * ab:2 * ab + 2] = v.reshape(2, 2, 32, 128)
+            R2s[r, 2 * ab:2 * ab + 2] = v.astype(BF16).reshape(2, 2, 32, 128)
         out = []
         for d, p in enumerate(zs_to):
             to = lax.rem(z + d + 1, 8)
-            out.append(send(R2s.at[f, lax.rem(to, 4), lax.div(to, 4)], R2r.at[f, d], p))
+            out.append(send(R2s.at[r, lax.rem(to, 4), lax.div(to, 4)], R2r.at[r, d], p))
         return out
 
-    def column_sum(f, r2):
-        acc[f, zh] = R2f[f, zl, zh]
-        acc[f, 1 - zh] = jnp.zeros((48, 128), F32)
+    def column_sum(r, r2):
+        acc[r, zh] = R2f[r, zl, zh]
+        acc[r, 1 - zh] = jnp.zeros((32, 128), F32)
         for d, cp in enumerate(r2):
             cp.wait_recv()
             half = lax.div(lax.rem(z + 7 - d, 8), 4)
-            acc[f, half] = acc[f, half] + R2r[f, d].astype(F32)
-
-    for q in (1, 2):
-        for cp in rs[q, None]:
-            cp.wait_recv()
-    r1a = near_scatter(0)
-    r1b = near_scatter(1)
-    weight_grads(3, 4)
-    r2a = column_scatter(0, r1a)
-    r2b = column_scatter(1, r1b)
-    weight_grads(4, 7)
-    column_sum(0, r2a)
-    column_sum(1, r2b)
-    theirs = pl.ds(pl.multiple_of((1 - c) * 24, 8), 24)
-    R3s[...] = jnp.concatenate(
-        [acc[f, h, theirs, :] for h in range(2) for f in range(2)], axis=0
-    ).astype(BF16)
+            acc[r, half] = acc[r, half] + R2r[r, d].astype(F32)
+        theirs = pl.ds(pl.multiple_of((1 - c) * 16, 16), 16)
+        for h in range(2):
+            R3s[r, h] = acc[r, h, theirs, :].astype(BF16)
+            at = pl.ds(pl.multiple_of(r * 64 + (h * 2 + c) * 16, 16), 16)
+            tscr[at, :] = acc[r, h, pl.ds(pl.multiple_of(c * 16, 16), 16), :]
+
+    r1 = [near_scatter(0, rs[1, None]), near_scatter(1, rs[2, None])]
+    transpose_acts()
+    weight_grads(0, 2)
+    r2 = [column_scatter(0, r1[0]), column_scatter(1, r1[1])]
+    r1.append(near_scatter(2, rs[3, 0] + rs[3, 1]))
+    weight_grads(2, 4)
+    column_sum(0, r2[0])
+    r2.append(column_scatter(2, r1[2]))
+    column_sum(1, r2[1])
+    weight_grads(4, 8)
+    write_hidden()
+    column_sum(2, r2[2])
     r3 = send(R3s, R3r, sib)
-    weight_grads(7, 8)
-    for h in range(2):
-        for f in range(2):
-            for r in range(3):
-                at = pl.ds(pl.multiple_of(r * 64 + (h * 2 + c) * 16 + f * 8, 8), 8)
-                tscr[at, :] = acc[f, h, pl.ds(pl.multiple_of(c * 24 + r * 8, 8), 8), :]
     r3.wait_recv()
-    R3f[...] = R3r[...].astype(F32)
-    for h in range(2):
-        for f in range(2):
-            for r in range(3):
-                at = pl.ds(pl.multiple_of(r * 64 + (h * 2 + 1 - c) * 16 + f * 8, 8), 8)
-                b = (h * 2 + f) * 24 + r * 8
-                tscr[at, :] = R3f[b:b + 8, :]
+    for r in range(3):
+        for h in range(2):
+            at = pl.ds(pl.multiple_of(r * 64 + (h * 2 + 1 - c) * 16, 16), 16)
+            tscr[at, :] = R3r[r, h].astype(F32)
     for j in range(64):
         token_out[:, j * 128:(j + 1) * 128] = tscr[pl.ds(j, 3, stride=64), :].astype(BF16)
 
     for cp in copies:
         cp.wait_send()
 
-    @pl.loop(0, 8)
-    def _(j):
-        cols = pl.ds(pl.multiple_of(j * 256, 256), 256)
-        pltpu.make_async_copy(GG.at[:, cols], gate_out.at[:, cols], out_sem.at[j, 0]).wait()
-        pltpu.make_async_copy(UG.at[:, cols], up_out.at[:, cols], out_sem.at[j, 1]).wait()
+
+def finish(*refs):
+    n = len(refs) // 2
+    sem = refs[-1]
+    copies = [pltpu.make_async_copy(refs[i], refs[n + i], sem.at[i]) for i in range(n)]
+    for cp in copies:
+        cp.start()
+    for cp in copies:
+        cp.wait()
 
 
 def on_device(tokens, gate_master, up_master, hidden_cotangent):
     vmem = pl.BlockSpec(memory_space=pltpu.VMEM)
     anywhere = pl.BlockSpec(memory_space=pl.ANY)
     V = pltpu.VMEM
-    n_copies = 128
-    hidden, token_grad, gate_grad, up_grad = pl.pallas_call(
+    n_copies = 136
+    shapes = ((192, FW), (3, 8192), (FW, DQ), (FW, DQ))
+    results = pl.pallas_call(
         kernel,
-        out_shape=(
-            jax.ShapeDtypeStruct((192, FW), BF16),
-            jax.ShapeDtypeStruct((3, 8192), BF16),
-            jax.ShapeDtypeStruct((FW, DQ), BF16),
-            jax.ShapeDtypeStruct((FW, DQ), BF16),
-        ),
+        out_shape=tuple(V(shape, BF16) for shape in shapes),
         in_specs=[vmem, anywhere, anywhere, vmem],
-        out_specs=(vmem, vmem, anywhere, anywhere),
+        out_specs=(vmem,) * 4,
         scratch_shapes=[
             V((2, 4, 2, 2, 2, 3, 16, 128), BF16),
             V((2, 2, 3, 16, 128), BF16),
@@ -466,30 +461,40 @@
             V((3, 2, 192, 1024), BF16),
             V((2, 192, 1024), F32),
             V((2, 2, 3, 96, 1024), BF16),
-            V((2, 2, 768, 128), F32),
-            V((2, 2, 4, 192, 128), BF16),
-            V((2, 2, 3, 192, 128), BF16),
-            V((2, 4, 2, 48, 128), F32),
-            V((2, 4, 2, 48, 128), BF16),
-            V((2, 7, 48, 128), BF16),
-            V((2, 2, 48, 128), F32),
-            V((96, 128), BF16),
-            V((96, 128), BF16),
-            V((96, 128), F32),
+            V((3, 2, 512, 128), F32),
+            V((3, 2, 4, 128, 128), BF16),
+            V((3, 2, 3, 128, 128), BF16),
+            V((3, 4, 2, 32, 128), F32),
+            V((3, 4, 2, 32, 128), BF16),
+            V((3, 7, 32, 128), BF16),
+            V((3, 2, 32, 128), F32),
+            V((3, 2, 16, 128), BF16),
+            V((3, 2, 16, 128), BF16),
             V((192, 128), F32),
             V((FP, 768), BF16),
-            V((FW, DQ), BF16),
-            V((FW, DQ), BF16),
             pltpu.SemaphoreType.DMA((4, 2)),
-            pltpu.SemaphoreType.DMA((8, 2)),
             pltpu.SemaphoreType.DMA((n_copies,)),
             pltpu.SemaphoreType.DMA((n_copies,)),
         ],
         compiler_params=pltpu.CompilerParams(
-            collective_id=0, has_side_effects=True, vmem_limit_bytes=58 * 2**20
+            collective_id=0, has_side_effects=True, vmem_limit_bytes=36 * 2**20
         ),
         name="swiglu_step",
-    )(tokens, gate_master.T, up_master.T, hidden_cotangent)
+    )(
+        tokens,
+        pltpu.with_memory_space_constraint(gate_master.T, pltpu.HBM),
+        pltpu.with_memory_space_constraint(up_master.T, pltpu.HBM),
+        hidden_cotangent,
+    )
+    hidden, token_grad, gate_grad, up_grad = pl.pallas_call(
+        finish,
+        out_shape=tuple(jax.ShapeDtypeStruct(shape, BF16) for shape in shapes),
+        in_specs=[vmem] * 4,
+        out_specs=(anywhere,) * 4,
+        scratch_shapes=[pltpu.SemaphoreType.DMA((4,))],
+        compiler_params=pltpu.CompilerParams(vmem_limit_bytes=8 * 2**20),
+        name="finish",
+    )(*(pltpu.with_memory_space_constraint(r, pltpu.VMEM) for r in results))
     return hidden, token_grad, gate_grad.T, up_grad.T
 
 

time: 104 us -> 103 us (level)
  local copies, waits for them, and re-layouts: 7.26 us -> 1.76 us
  Pallas kernels: 95.4 us -> 100 us
    unnamed x6 -> x4, local copies, waits for them, and re-layouts: 7.26 us -> 1.76 us
    pallas_call x1 -> x2, Pallas kernels: 95.4 us -> 100 us  [the longest x1 98.1 us: on_device(): pl.pallas_call(kernel, out_shape=tuple((V(shape, BF16) for shape in shape...]
where the time goes in v3:
time: 103 us; the launch traced here: 102 us
  Pallas kernels  100 us (97%)
  local copies, waits for them, and re-layouts  1.76 us (2%)
    pallas_call x1, Pallas kernels, on_device(): pl.pallas_call(kernel, out_shape=tuple((V(shape, BF16) for shape in shape...  98.1 us

profile of v3, /device:TPU:1, one launch (start us, length us, event | category | flops | bytes accessed | tf_op | source)
XLA Modules:
  0.0 102.4 jit_solution(9969979215998311959)
XLA Ops:
  0.6 0.0 copy-start
  0.6 0.9 copy-done
  1.6 0.0 copy-start.1
  1.6 0.8 copy-done.1
  2.4 98.1 %swiglu_step.1 = (bf16[192,416]{1,0:T(8,128)(2,1)S(1)}, bf16[3,8192]{1,0:T(4,128)(2,1)S(1)}, bf16[416,2048]{1,0:T(8,128)(2,1)S(1)}, bf16[416,2048]{1,0:T(8,128)(2,1)S(1)}) custom-call(bf16[3,8192]{1,0:T(4,128)(2,1)S(1)} %copy-done.1, bf16[416,2048]{1,0:T(8,128)(2,1)} %bitcast.4, bf16[416,2048]{1,0:T(8,128)(2,1)} %bitcast.5, bf16[192,416]{1,0:T(8,128)(2,1)S(1)} %copy-done), custom_call_target="tpu_custom_call" | custom-call | tf_op jit(solution)/shard_map/swiglu_step/pallas_call | solution.py:435
  100.5 1.9 %finish.1 = (bf16[192,416]{1,0:T(8,128)(2,1)}, bf16[3,8192]{1,0:T(4,128)(2,1)}, bf16[416,2048]{1,0:T(8,128)(2,1)}, bf16[416,2048]{1,0:T(8,128)(2,1)}) custom-call(bf16[192,416]{1,0:T(8,128)(2,1)S(1)} %get-tuple-element.12.refs_0_, bf16[3,8192]{1,0:T(4,128)(2,1)S(1)} %get-tuple-element.13.refs_1_, bf16[416,2048]{1,0:T(8,128)(2,1)S(1)} %get-tuple-element.14.refs_2_, ...), custom_call_target="tpu_custom_call" | custom-call | tf_op jit(solution)/shard_map/finish/pallas_call | solution.py:489
Async XLA Ops:
  0.6 0.9 copy-start
  1.6 0.8 copy-start.1

commit v4 on v3

--- a/solution.py
+++ b/solution.py
@@ -45,12 +45,12 @@
 
 
 def kernel(
-    tokens, gate_hbm, up_hbm, cot,
+    tokens_hbm, gate_hbm, up_hbm, cot_hbm,
     hidden_out, token_out, GG, UG,
-    S, tokb, TK, scr, X, Wt, gm, um, am_tx, am_rx, cotf,
-    Pf, Ps, Pr, Qs, Qr, Ag, Ax, Asc, H, TS, TO, RT, scr2, R1s, R1r, R2f, R2s, R2r, acc, R3s, R3r, tscr,
+    tokens, cot, S, tokb, TK, scr, X, Wt, gm, um, am_tx, am_rx, cotp, cotr, cotf,
+    Pf, Ps, Pr, Q0s, Q0r, Qs, Qr, Ag, Ax, Asc, H, TS, TO, RT, scr2, R1s, R1r, R2f, R2s, R2r, acc, R3s, R3r, tscr,
     At,
-    load_sem, tx, rx,
+    load_sem, in_sem, tx, rx,
 ):
     zh, c, y, zl, x = position()
     sib = place(zh, 1 - c, y, zl, x)
@@ -84,6 +84,10 @@
         copies.append(cp)
         return cp
 
+    small = []
+    for i, (src, dst) in enumerate(((tokens_hbm, tokens), (cot_hbm, cot))):
+        small.append(pltpu.make_async_copy(src, dst, in_sem.at[i]))
+        small[i].start()
     loads = []
     for i, (start, count) in enumerate(LOADS):
         rows = pl.ds(start, count)
@@ -96,6 +100,7 @@
     for p in peers:
         pl.semaphore_signal(barrier, inc=1, device_id=p, device_id_type=MESH)
 
+    small[0].wait()
     for j in range(64):
         tscr[pl.ds(j, 3, stride=64), :] = tokens[:, j * 128:(j + 1) * 128].astype(F32)
     for g in range(4):
@@ -142,10 +147,13 @@
     merge(0, 0, m)
     m = share(1, 1, xs_to)
 
+    small[1].wait()
     mine = absolute_row(lax.broadcasted_iota(jnp.int32, (192, 1), 0), y, x)
     col = lax.broadcasted_iota(jnp.int32, (192, 192), 1)
     pick = (col == mine).astype(F32).astype(BF16)
-    cotf[...] = jnp.dot(pick, cot[...], preferred_element_type=F32)
+    cperm = jnp.dot(pick, cot[...], preferred_element_type=F32)
+    cotf[zh] = cperm
+    cotp[...] = cperm.astype(BF16)
     merge(1, 1, m)
     m = share(2, 4, ys_to)
     merge(2, 4, m)
@@ -157,6 +165,8 @@
         s2[0].append(send(S.at[0, 0], S.at[0, d], at_x(4 - d)))
         s2[1].append(send(S.at[1, 0], S.at[1, d], at_y(4 - d)))
     merge(3, 7, m)
+    remote = pl.ds(48, 144)
+    cot_copy = send(cotp.at[remote], cotr.at[remote], anti)
 
     g_amax = jnp.max(am_tx[4, 0:8, :], axis=(0, 1), keepdims=True)
     u_amax = jnp.max(am_tx[4, 8:16, :], axis=(0, 1), keepdims=True)
@@ -217,24 +227,47 @@
 
     def cross(q):
         p_copies[q].wait_recv()
-        Qs[q] = (Pf[q, c, 1 - zh] + Pr[q, 1 - zh].astype(F32)).astype(BF16)
-        q_copies[q] = send(Qs.at[q], Qr.at[q], anti)
-
-    def act(q):
-        own = Pf[q, c, zh] + Pr[q, zh].astype(F32)
-        q_copies[q].wait_recv()
-        pre = own + Qr[q].astype(F32)
+        if q == 0:
+            Q0s[...] = (Pf[q, c, 1 - zh] + Pr[q, 1 - zh].astype(F32)).astype(BF16)
+            q_copies[q] = send(Q0s, Q0r, anti)
+        else:
+            tails = []
+            for h in range(2):
+                v = Pf[q, c, h] + Pr[q, h].astype(F32)
+                for j in range(6):
+                    Qs[q - 1, h * 6 + j] = v[:, j * 128:(j + 1) * 128].astype(BF16)
+                tails.append(v[:, 2 * FA:])
+            Qs[q - 1, 12] = jnp.concatenate(tails, axis=1).astype(BF16)
+            q_copies[q] = send(Qs.at[q - 1], Qr.at[q - 1], anti)
+
+    def act_rows(q, h):
+        pre = Pf[q, c, h] + Pr[q, h].astype(F32)
+        if q == 0:
+            pre = pre + Q0r[...].astype(F32)
+        else:
+            tail = Qr[q - 1, 12].astype(F32)[:, h * 2 * FT:(h + 1) * 2 * FT]
+            tiles = [Qr[q - 1, h * 6 + j].astype(F32) for j in range(6)]
+            pre = pre + jnp.concatenate(tiles + [tail], axis=1)
         gate = jnp.concatenate([pre[:, :FA], pre[:, 2 * FA:2 * FA + FT]], axis=1) * g_scale
         up = jnp.concatenate([pre[:, FA:2 * FA], pre[:, 2 * FA + FT:FP]], axis=1) * u_scale
-        cotangent = cotf[q * 48:q * 48 + 48, :]
+        cotangent = cotf[h, q * 48:q * 48 + 48, :]
         sig = jax.nn.sigmoid(gate)
         silu = gate * sig
-        H[q * 48:q * 48 + 48, :] = (silu * up).astype(BF16)
+        H[h, q * 48:q * 48 + 48, :] = (silu * up).astype(BF16)
         ga = cotangent * up * sig * (1.0 + gate * (1.0 - sig))
         ua = cotangent * silu
         packed = jnp.concatenate([ga[:, :FA], ua[:, :FA], ga[:, FA:], ua[:, FA:]], axis=1)
-        Ag[q, c, zh] = packed.astype(BF16)
-        sib_copies[q] = send(Ag.at[q, c, zh], Ag.at[q, c, zh], sib)
+        Ag[q, c, h] = packed.astype(BF16)
+
+    def act(q):
+        q_copies[q].wait_recv()
+        if q == 0:
+            act_rows(q, zh)
+            sib_copies[q] = send(Ag.at[q, c, zh], Ag.at[q, c, zh], sib)
+        else:
+            for h in range(2):
+                act_rows(q, h)
+            sib_copies[q] = send(Ag.at[q, c], Ag.at[q, c], sib)
 
     def cross_back(q):
         anti_copies[q] = send(Ag.at[q, c, zh], Ag.at[q, c, zh], anti)
@@ -250,7 +283,8 @@
 
     def backward(q):
         sib_copies[q].wait_recv()
-        fwd_copies[q].wait_recv()
+        if q == 0:
+            fwd_copies[q].wait_recv()
         parts = [Ag[q, k // 2, k % 2].astype(F32) for k in range(4)]
         rows = jnp.concatenate(
             [parts[k][i * 8:i * 8 + 8] for i in range(6) for k in range(4)], axis=0
@@ -285,6 +319,10 @@
                     send(TS.at[q - 1, fs, here], RT.at[fs, ab, d - 1, there], far(ab)(d))
                 )
 
+    def transpose_acts(blocks):
+        for i in blocks:
+            At[:, i * 128:(i + 1) * 128] = Ax[...].reshape(768, FP)[i * 128:(i + 1) * 128, :].T
+
     gather(1)
     forward(0)
     gather(2)
@@ -295,39 +333,32 @@
     gather(3)
     cross(1)
     act(0)
-    cross_back(0)
     for cp in big[2]:
         cp.wait_recv()
     forward(2)
     cross(2)
+    cot_copy.wait_recv()
+    cotf[1 - zh, remote, :] = cotr[remote, :].astype(F32)
     act(1)
-    cross_back(1)
     for cp in big[3]:
         cp.wait_recv()
     forward(3)
     cross(3)
+    cross_back(0)
+    backward(1)
+    act(2)
+    backward(2)
+    transpose_acts((2, 3))
+    act(3)
+    backward(3)
     pass_on(0)
-    act(2)
-    cross_back(2)
     backward(0)
-    pass_on(1)
-    backward(1)
-    act(3)
-    cross_back(3)
-    pass_on(2)
-    backward(2)
-    pass_on(3)
-    backward(3)
 
     def write_hidden():
         row = lax.broadcasted_iota(jnp.int32, (192, 192), 0)
         there = absolute_row(lax.broadcasted_iota(jnp.int32, (1, 192), 1), y, x)
         pick = (row == there).astype(F32).astype(BF16)
-        hidden_out[...] = jnp.dot(pick, H[...], preferred_element_type=F32).astype(BF16)
-
-    def transpose_acts():
-        for i in range(6):
-            At[:, i * 128:(i + 1) * 128] = Ax[...].reshape(768, FP)[i * 128:(i + 1) * 128, :].T
+        hidden_out[...] = jnp.dot(pick, H[zh], preferred_element_type=F32).astype(BF16)
 
     def weight_grads(first, last):
         @pl.loop(first, last)
@@ -392,16 +423,17 @@
             tscr[at, :] = acc[r, h, pl.ds(pl.multiple_of(c * 16, 16), 16), :]
 
     r1 = [near_scatter(0, rs[1, None]), near_scatter(1, rs[2, None])]
-    transpose_acts()
-    weight_grads(0, 2)
-    r2 = [column_scatter(0, r1[0]), column_scatter(1, r1[1])]
+    transpose_acts((0, 1, 4, 5))
+    weight_grads(0, 3)
+    r2 = [column_scatter(0, r1[0])]
     r1.append(near_scatter(2, rs[3, 0] + rs[3, 1]))
-    weight_grads(2, 4)
+    r2.append(column_scatter(1, r1[1]))
+    weight_grads(3, 6)
+    r2.append(column_scatter(2, r1[2]))
     column_sum(0, r2[0])
-    r2.append(column_scatter(2, r1[2]))
+    weight_grads(6, 8)
+    write_hidden()
     column_sum(1, r2[1])
-    weight_grads(4, 8)
-    write_hidden()
     column_sum(2, r2[2])
     r3 = send(R3s, R3r, sib)
     r3.wait_recv()
@@ -435,9 +467,11 @@
     results = pl.pallas_call(
         kernel,
         out_shape=tuple(V(shape, BF16) for shape in shapes),
-        in_specs=[vmem, anywhere, anywhere, vmem],
+        in_specs=[anywhere] * 4,
         out_specs=(vmem,) * 4,
         scratch_shapes=[
+            V((3, 8192), BF16),
+            V((192, FW), BF16),
             V((2, 4, 2, 2, 2, 3, 16, 128), BF16),
             V((2, 2, 3, 16, 128), BF16),
             V((2, 2, 3, 16, 128), BF16),
@@ -448,16 +482,20 @@
             V((FW, DQ), BF16),
             V((5, 16, 128), F32),
             V((14, 16, 128), F32),
-            V((192, FW), F32),
+            V((192, FW), BF16),
+            V((192, FW), BF16),
+            V((2, 192, FW), F32),
             V((4, 2, 2, 48, FP), F32),
             V((4, 2, 48, FP), BF16),
             V((4, 2, 48, FP), BF16),
-            V((4, 48, FP), BF16),
-            V((4, 48, FP), BF16),
+            V((48, FP), BF16),
+            V((48, FP), BF16),
+            V((3, 13, 48, 128), BF16),
+            V((3, 13, 48, 128), BF16),
             V((4, 2, 2, 48, FP), BF16),
             V((4, 192, FP), BF16),
             V((192, FP), BF16),
-            V((192, FW), BF16),
+            V((2, 192, FW), BF16),
             V((3, 2, 192, 1024), BF16),
             V((2, 192, 1024), F32),
             V((2, 2, 3, 96, 1024), BF16),
@@ -473,6 +511,7 @@
             V((192, 128), F32),
             V((FP, 768), BF16),
             pltpu.SemaphoreType.DMA((4, 2)),
+            pltpu.SemaphoreType.DMA((2,)),
             pltpu.SemaphoreType.DMA((n_copies,)),
             pltpu.SemaphoreType.DMA((n_copies,)),
         ],
@@ -481,10 +520,10 @@
         ),
         name="swiglu_step",
     )(
-        tokens,
-        pltpu.with_memory_space_constraint(gate_master.T, pltpu.HBM),
-        pltpu.with_memory_space_constraint(up_master.T, pltpu.HBM),
-        hidden_cotangent,
+        *(
+            pltpu.with_memory_space_constraint(a, pltpu.HBM)
+            for a in (tokens, gate_master.T, up_master.T, hidden_cotangent)
+        )
     )
     hidden, token_grad, gate_grad, up_grad = pl.pallas_call(
         finish,

time: 103 us -> 93.6 us (0.909)
  Pallas kernels: 100 us -> 92.8 us
  local copies, waits for them, and re-layouts: 1.76 us -> 0 us
    pallas_call x1, Pallas kernels: 98.1 us -> 91 us  [on_device(): pl.pallas_call(kernel, out_shape=tuple((V(shape, BF16) for shape in shape...]
    unnamed x4 -> x0, local copies, waits for them, and re-layouts: 1.76 us -> none
where the time goes in v4:
time: 93.6 us; the launch traced here: 93.5 us
  Pallas kernels  92.8 us (99%)
    pallas_call x1, Pallas kernels, on_device(): pl.pallas_call(kernel, out_shape=tuple((V(shape, BF16) for shape in shape...  91 us

profile of v4, /device:TPU:1, one launch (start us, length us, event | category | flops | bytes accessed | tf_op | source)
XLA Modules:
  0.0 93.5 jit_solution(8821450581644908835)
XLA Ops:
  0.6 91.0 %swiglu_step.1 = (bf16[192,416]{1,0:T(8,128)(2,1)S(1)}, bf16[3,8192]{1,0:T(4,128)(2,1)S(1)}, bf16[416,2048]{1,0:T(8,128)(2,1)S(1)}, bf16[416,2048]{1,0:T(8,128)(2,1)S(1)}) custom-call(bf16[3,8192]{1,0:T(4,128)(2,1)} %tokens_hbm.1, bf16[416,2048]{1,0:T(8,128)(2,1)} %bitcast.4, bf16[416,2048]{1,0:T(8,128)(2,1)} %bitcast.5, bf16[192,416]{1,0:T(8,128)(2,1)} %cot_hbm.1), custom_call_target="tpu_custom_call" | custom-call | tf_op jit(solution)/shard_map/swiglu_step/pallas_call | solution.py:467
  91.6 1.9 %finish.1 = (bf16[192,416]{1,0:T(8,128)(2,1)}, bf16[3,8192]{1,0:T(4,128)(2,1)}, bf16[416,2048]{1,0:T(8,128)(2,1)}, bf16[416,2048]{1,0:T(8,128)(2,1)}) custom-call(bf16[192,416]{1,0:T(8,128)(2,1)S(1)} %get-tuple-element.12.refs_0_, bf16[3,8192]{1,0:T(4,128)(2,1)S(1)} %get-tuple-element.13.refs_1_, bf16[416,2048]{1,0:T(8,128)(2,1)S(1)} %get-tuple-element.14.refs_2_, ...), custom_call_target="tpu_custom_call" | custom-call | tf_op jit(solution)/shard_map/finish/pallas_call | solution.py:528

commit v5 on v4

--- a/solution.py
+++ b/solution.py
@@ -35,10 +35,12 @@
 
 def absolute_row(n, y, x):
     chunk, i, u = lax.div(n, 48), lax.div(lax.rem(n, 48), 8), lax.rem(n, 8)
-    ab, three = lax.div(i, 3), lax.rem(i, 3)
+    own = chunk == 0
+    ab = jnp.where(own, lax.div(i, 3), lax.rem(i, 2))
+    three = jnp.where(own, lax.rem(i, 3), lax.div(i, 2))
     near, zls = lax.div(u, 2), lax.rem(u, 2)
-    d = jnp.where(chunk == 0, 0, jnp.where(three == 0, FAR[0], jnp.where(three == 1, FAR[1], FAR[2])))
-    r = jnp.where(chunk == 0, three, chunk - 1)
+    d = jnp.where(own, 0, jnp.where(three == 0, FAR[0], jnp.where(three == 1, FAR[1], FAR[2])))
+    r = jnp.where(own, three, chunk - 1)
     row_a = lax.rem(y + d, 4) * 16 + zls * 4 + lax.rem(x + near, 4)
     row_b = lax.rem(y + near, 4) * 16 + (zls + 2) * 4 + lax.rem(x + d, 4)
     return jnp.where(ab == 0, row_a, row_b) * 3 + r
@@ -207,67 +209,76 @@
         for t, d in enumerate(FAR):
             for ab in range(2):
                 own = pl.ds(ab * 96 + (q - 1) * 32, 32)
-                there = pl.ds((ab * 3 + t) * 32, 32)
+                there = pl.ds((t * 2 + ab) * 32, 32)
                 big[q].append(send(X.at[0, own], X.at[q, there], far(ab)(4 - d)))
 
     p_copies, q_copies, sib_copies, anti_copies, fwd_copies = {}, {}, {}, {}, {}
 
-    def forward(q):
+    def forward(q, first=0, last=6):
+        if q > 0:
+            for cp in big[q][first:last]:
+                cp.wait_recv()
         for n in range(0, FP, 256):
             width = min(256, FP - n)
             part = lax.dot_general(
-                X[q], Wt[n:n + width, :], (((1,), (1,)), ((), ())), preferred_element_type=F32
+                X[q, first * 32:last * 32, :], Wt[n:n + width, :],
+                (((1,), (1,)), ((), ())), preferred_element_type=F32,
             )
-            for i in range(6):
+            for i in range(first, last):
                 for k in range(4):
-                    at = (i * 4 + k) * 8
+                    at = ((i - first) * 4 + k) * 8
                     Pf[q, k // 2, k % 2, i * 8:i * 8 + 8, n:n + width] = part[at:at + 8]
-        Ps[q] = Pf[q, 1 - c].astype(BF16)
-        p_copies[q] = send(Ps.at[q], Pr.at[q], sib)
-
-    def cross(q):
-        p_copies[q].wait_recv()
+        rows = pl.ds(first * 8, (last - first) * 8)
+        Ps[q, :, rows, :] = Pf[q, 1 - c, :, rows, :].astype(BF16)
+        p_copies[q, first] = send(Ps.at[q, :, rows], Pr.at[q, :, rows], sib)
+
+    def cross(q, first=0, last=6):
+        p_copies[q, first].wait_recv()
+        rows = pl.ds(first * 8, (last - first) * 8)
         if q == 0:
             Q0s[...] = (Pf[q, c, 1 - zh] + Pr[q, 1 - zh].astype(F32)).astype(BF16)
-            q_copies[q] = send(Q0s, Q0r, anti)
+            q_copies[q, first] = send(Q0s, Q0r, anti)
         else:
             tails = []
             for h in range(2):
-                v = Pf[q, c, h] + Pr[q, h].astype(F32)
+                v = Pf[q, c, h, rows, :] + Pr[q, h, rows, :].astype(F32)
                 for j in range(6):
-                    Qs[q - 1, h * 6 + j] = v[:, j * 128:(j + 1) * 128].astype(BF16)
+                    Qs[q - 1, h * 6 + j, rows, :] = v[:, j * 128:(j + 1) * 128].astype(BF16)
                 tails.append(v[:, 2 * FA:])
-            Qs[q - 1, 12] = jnp.concatenate(tails, axis=1).astype(BF16)
-            q_copies[q] = send(Qs.at[q - 1], Qr.at[q - 1], anti)
-
-    def act_rows(q, h):
-        pre = Pf[q, c, h] + Pr[q, h].astype(F32)
+            Qs[q - 1, 12, rows, :] = jnp.concatenate(tails, axis=1).astype(BF16)
+            q_copies[q, first] = send(Qs.at[q - 1, :, rows], Qr.at[q - 1, :, rows], anti)
+
+    def act_rows(q, h, first, last):
+        rows = pl.ds(first * 8, (last - first) * 8)
+        pre = Pf[q, c, h, rows, :] + Pr[q, h, rows, :].astype(F32)
         if q == 0:
             pre = pre + Q0r[...].astype(F32)
         else:
-            tail = Qr[q - 1, 12].astype(F32)[:, h * 2 * FT:(h + 1) * 2 * FT]
-            tiles = [Qr[q - 1, h * 6 + j].astype(F32) for j in range(6)]
+            tail = Qr[q - 1, 12, rows, :].astype(F32)[:, h * 2 * FT:(h + 1) * 2 * FT]
+            tiles = [Qr[q - 1, h * 6 + j, rows, :].astype(F32) for j in range(6)]
             pre = pre + jnp.concatenate(tiles + [tail], axis=1)
         gate = jnp.concatenate([pre[:, :FA], pre[:, 2 * FA:2 * FA + FT]], axis=1) * g_scale
         up = jnp.concatenate([pre[:, FA:2 * FA], pre[:, 2 * FA + FT:FP]], axis=1) * u_scale
-        cotangent = cotf[h, q * 48:q * 48 + 48, :]
+        mine = pl.ds(q * 48 + first * 8, (last - first) * 8)
+        cotangent = cotf[h, mine, :]
         sig = jax.nn.sigmoid(gate)
         silu = gate * sig
-        H[h, q * 48:q * 48 + 48, :] = (silu * up).astype(BF16)
+        H[h, mine, :] = (silu * up).astype(BF16)
         ga = cotangent * up * sig * (1.0 + gate * (1.0 - sig))
         ua = cotangent * silu
         packed = jnp.concatenate([ga[:, :FA], ua[:, :FA], ga[:, FA:], ua[:, FA:]], axis=1)
-        Ag[q, c, h] = packed.astype(BF16)
-
-    def act(q):
-        q_copies[q].wait_recv()
+        Ag[q, c, h, rows, :] = packed.astype(BF16)
+
+    def act(q, first=0, last=6):
+        q_copies[q, first].wait_recv()
         if q == 0:
-            act_rows(q, zh)
-            sib_copies[q] = send(Ag.at[q, c, zh], Ag.at[q, c, zh], sib)
+            act_rows(q, zh, first, last)
+            mine = Ag.at[q, c, zh]
         else:
             for h in range(2):
-                act_rows(q, h)
-            sib_copies[q] = send(Ag.at[q, c], Ag.at[q, c], sib)
+                act_rows(q, h, first, last)
+            mine = Ag.at[q, c, :, pl.ds(first * 8, (last - first) * 8)]
+        sib_copies[q, first] = send(mine, mine, sib)
 
     def cross_back(q):
         anti_copies[q] = send(Ag.at[q, c, zh], Ag.at[q, c, zh], anti)
@@ -279,45 +290,45 @@
     lane = lax.broadcasted_iota(jnp.int32, (1, FP), 1)
     is_gate = (lane < FA) | ((lane >= 2 * FA) & (lane < 2 * FA + FT))
     scale_row = jnp.where(is_gate, g_scale, u_scale)
-    rs = {}
-
-    def backward(q):
-        sib_copies[q].wait_recv()
+    rs = {1: [], 2: [], 3: []}
+
+    def backward(q, first=0, last=6):
+        for f in range(first, last):
+            if (q, f) in sib_copies:
+                sib_copies[q, f].wait_recv()
         if q == 0:
             fwd_copies[q].wait_recv()
-        parts = [Ag[q, k // 2, k % 2].astype(F32) for k in range(4)]
+        mine = pl.ds(first * 8, (last - first) * 8)
+        parts = [Ag[q, k // 2, k % 2, mine, :].astype(F32) for k in range(4)]
         rows = jnp.concatenate(
-            [parts[k][i * 8:i * 8 + 8] for i in range(6) for k in range(4)], axis=0
+            [parts[k][i * 8:i * 8 + 8] for i in range(last - first) for k in range(4)], axis=0
         )
-        Ax[q] = rows.astype(BF16)
-        Asc[...] = (rows * scale_row).astype(BF16)
+        here = pl.ds(first * 32, (last - first) * 32)
+        Ax[q, here, :] = rows.astype(BF16)
+        Asc[here, :] = (rows * scale_row).astype(BF16)
         for f in range(2):
 
             @pl.loop(0, 4)
             def _(j):
                 cols = pl.ds(pl.multiple_of(j * 256, 256), 256)
                 from_ = pl.ds(pl.multiple_of(f * 1024 + j * 256, 256), 256)
-                part = jnp.dot(Asc[...], Wt[:, from_], preferred_element_type=F32)
+                part = jnp.dot(Asc[here, :], Wt[:, from_], preferred_element_type=F32)
                 if q == 0:
                     TO[f, :, cols] = part
                 else:
-                    TS[q - 1, f, :, cols] = part.astype(BF16)
+                    TS[q - 1, f, here, cols] = part.astype(BF16)
 
             if q == 3:
-                scatter(q, f)
+                scatter(q, f, first, last)
         if q in (1, 2):
-            scatter(q, None)
-
-    def scatter(q, f):
-        fs = slice(None) if f is None else f
-        rs[q, f] = []
-        for t, d in enumerate(FAR):
-            for ab in range(2):
-                here = pl.ds((ab * 3 + t) * 32, 32)
-                there = pl.ds((q - 1) * 32, 32)
-                rs[q, f].append(
-                    send(TS.at[q - 1, fs, here], RT.at[fs, ab, d - 1, there], far(ab)(d))
-                )
+            scatter(q, slice(None), first, last)
+
+    def scatter(q, f, first, last):
+        for i in range(first, last):
+            d, ab = FAR[i // 2], i % 2
+            here = pl.ds(i * 32, 32)
+            there = pl.ds((q - 1) * 32, 32)
+            rs[q].append(send(TS.at[q - 1, f, here], RT.at[f, ab, d - 1, there], far(ab)(d)))
 
     def transpose_acts(blocks):
         for i in blocks:
@@ -327,30 +338,31 @@
     forward(0)
     gather(2)
     cross(0)
-    for cp in big[1]:
-        cp.wait_recv()
-    forward(1)
+    forward(1, 0, 4)
+    cross(1, 0, 4)
+    forward(1, 4, 6)
     gather(3)
-    cross(1)
+    cross(1, 4, 6)
     act(0)
-    for cp in big[2]:
-        cp.wait_recv()
     forward(2)
     cross(2)
     cot_copy.wait_recv()
     cotf[1 - zh, remote, :] = cotr[remote, :].astype(F32)
-    act(1)
-    for cp in big[3]:
-        cp.wait_recv()
-    forward(3)
-    cross(3)
+    act(1, 0, 4)
+    act(1, 4, 6)
+    forward(3, 0, 4)
+    cross(3, 0, 4)
+    forward(3, 4, 6)
+    cross(3, 4, 6)
     cross_back(0)
     backward(1)
     act(2)
     backward(2)
     transpose_acts((2, 3))
-    act(3)
-    backward(3)
+    act(3, 0, 4)
+    backward(3, 0, 4)
+    act(3, 4, 6)
+    backward(3, 4, 6)
     pass_on(0)
     backward(0)
 
@@ -422,20 +434,16 @@
             at = pl.ds(pl.multiple_of(r * 64 + (h * 2 + c) * 16, 16), 16)
             tscr[at, :] = acc[r, h, pl.ds(pl.multiple_of(c * 16, 16), 16), :]
 
-    r1 = [near_scatter(0, rs[1, None]), near_scatter(1, rs[2, None])]
+    r1 = [near_scatter(r, rs[r + 1]) for r in range(3)]
     transpose_acts((0, 1, 4, 5))
-    weight_grads(0, 3)
-    r2 = [column_scatter(0, r1[0])]
-    r1.append(near_scatter(2, rs[3, 0] + rs[3, 1]))
-    r2.append(column_scatter(1, r1[1]))
-    weight_grads(3, 6)
-    r2.append(column_scatter(2, r1[2]))
-    column_sum(0, r2[0])
+    weight_grads(0, 2)
+    r2 = [column_scatter(r, r1[r]) for r in range(3)]
+    weight_grads(2, 6)
+    for r in range(3):
+        column_sum(r, r2[r])
+    r3 = send(R3s, R3r, sib)
     weight_grads(6, 8)
     write_hidden()
-    column_sum(1, r2[1])
-    column_sum(2, r2[2])
-    r3 = send(R3s, R3r, sib)
     r3.wait_recv()
     for r in range(3):
         for h in range(2):
@@ -462,7 +470,7 @@
     vmem = pl.BlockSpec(memory_space=pltpu.VMEM)
     anywhere = pl.BlockSpec(memory_space=pl.ANY)
     V = pltpu.VMEM
-    n_copies = 136
+    n_copies = 144
     shapes = ((192, FW), (3, 8192), (FW, DQ), (FW, DQ))
     results = pl.pallas_call(
         kernel,

time: 93.6 us -> 93.7 us (level)
  no operation moved by 1% of the time
where the time goes in v5:
time: 93.7 us; the launch traced here: 93.6 us
  Pallas kernels  92.9 us (99%)
    pallas_call x1, Pallas kernels, on_device(): pl.pallas_call(kernel, out_shape=tuple((V(shape, BF16) for shape in shape...  91.1 us

profile of v5, /device:TPU:1, one launch (start us, length us, event | category | flops | bytes accessed | tf_op | source)
XLA Modules:
  0.0 93.6 jit_solution(4265142200162573168)
XLA Ops:
  0.6 91.1 %swiglu_step.1 = (bf16[192,416]{1,0:T(8,128)(2,1)S(1)}, bf16[3,8192]{1,0:T(4,128)(2,1)S(1)}, bf16[416,2048]{1,0:T(8,128)(2,1)S(1)}, bf16[416,2048]{1,0:T(8,128)(2,1)S(1)}) custom-call(bf16[3,8192]{1,0:T(4,128)(2,1)} %tokens_hbm.1, bf16[416,2048]{1,0:T(8,128)(2,1)} %bitcast.4, bf16[416,2048]{1,0:T(8,128)(2,1)} %bitcast.5, bf16[192,416]{1,0:T(8,128)(2,1)} %cot_hbm.1), custom_call_target="tpu_custom_call" | custom-call | tf_op jit(solution)/shard_map/swiglu_step/pallas_call | solution.py:475
  91.7 1.9 %finish.1 = (bf16[192,416]{1,0:T(8,128)(2,1)}, bf16[3,8192]{1,0:T(4,128)(2,1)}, bf16[416,2048]{1,0:T(8,128)(2,1)}, bf16[416,2048]{1,0:T(8,128)(2,1)}) custom-call(bf16[192,416]{1,0:T(8,128)(2,1)S(1)} %get-tuple-element.12.refs_0_, bf16[3,8192]{1,0:T(4,128)(2,1)S(1)} %get-tuple-element.13.refs_1_, bf16[416,2048]{1,0:T(8,128)(2,1)S(1)} %get-tuple-element.14.refs_2_, ...), custom_call_target="tpu_custom_call" | custom-call | tf_op jit(solution)/shard_map/finish/pallas_call | solution.py:536

commit v6 on v5

--- a/solution.py
+++ b/solution.py
@@ -351,14 +351,15 @@
     act(1, 0, 4)
     act(1, 4, 6)
     forward(3, 0, 4)
+    backward(1)
     cross(3, 0, 4)
     forward(3, 4, 6)
     cross(3, 4, 6)
     cross_back(0)
-    backward(1)
     act(2)
+    transpose_acts((2,))
     backward(2)
-    transpose_acts((2, 3))
+    transpose_acts((3,))
     act(3, 0, 4)
     backward(3, 0, 4)
     act(3, 4, 6)

time: 93.7 us -> 92.2 us (0.984)
  Pallas kernels: 92.9 us -> 91.5 us
    pallas_call x1, Pallas kernels: 91.1 us -> 89.6 us  [on_device(): pl.pallas_call(kernel, out_shape=tuple((V(shape, BF16) for shape in shape...]
where the time goes in v6:
time: 92.2 us; the launch traced here: 92.1 us
  Pallas kernels  91.5 us (99%)
    pallas_call x1, Pallas kernels, on_device(): pl.pallas_call(kernel, out_shape=tuple((V(shape, BF16) for shape in shape...  89.6 us
    pallas_call x1, Pallas kernels, on_device(): pl.pallas_call(finish, out_shape=tuple((jax.ShapeDtypeStruct(shape, BF16)...  1.87 us

profile of v6, /device:TPU:1, one launch (start us, length us, event | category | flops | bytes accessed | tf_op | source)
XLA Modules:
  0.0 92.1 jit_solution(16053570397913252371)
XLA Ops:
  0.6 89.6 %swiglu_step.1 = (bf16[192,416]{1,0:T(8,128)(2,1)S(1)}, bf16[3,8192]{1,0:T(4,128)(2,1)S(1)}, bf16[416,2048]{1,0:T(8,128)(2,1)S(1)}, bf16[416,2048]{1,0:T(8,128)(2,1)S(1)}) custom-call(bf16[3,8192]{1,0:T(4,128)(2,1)} %tokens_hbm.1, bf16[416,2048]{1,0:T(8,128)(2,1)} %bitcast.4, bf16[416,2048]{1,0:T(8,128)(2,1)} %bitcast.5, bf16[192,416]{1,0:T(8,128)(2,1)} %cot_hbm.1), custom_call_target="tpu_custom_call" | custom-call | tf_op jit(solution)/shard_map/swiglu_step/pallas_call | solution.py:476
  90.2 1.9 %finish.1 = (bf16[192,416]{1,0:T(8,128)(2,1)}, bf16[3,8192]{1,0:T(4,128)(2,1)}, bf16[416,2048]{1,0:T(8,128)(2,1)}, bf16[416,2048]{1,0:T(8,128)(2,1)}) custom-call(bf16[192,416]{1,0:T(8,128)(2,1)S(1)} %get-tuple-element.12.refs_0_, bf16[3,8192]{1,0:T(4,128)(2,1)S(1)} %get-tuple-element.13.refs_1_, bf16[416,2048]{1,0:T(8,128)(2,1)S(1)} %get-tuple-element.14.refs_2_, ...), custom_call_target="tpu_custom_call" | custom-call | tf_op jit(solution)/shard_map/finish/pallas_call | solution.py:537
